TPU v7x, 32 devices: a whole 2x2x4 slice. The times are simulated.
32 devices in a mesh: orb: 8 (over z, core), dom: 4 (over y, x).
Axes of the slice: x: 2, y: 2, z: 4, core: 2. Of those that a mesh axis runs over, the one named last changes fastest.
Arguments:
- orbitals: bfloat16 [8, 16, 48, 128], P('orb', None, 'dom'), may hold values from -6 to 6
- potential: float32 [16, 48, 128], P(None, 'dom'), may hold values from 0 to 2
- degree: int32 [8], P('orb'), may hold values from 1 to 8, as said below
- owners: int32 [4], replicated, may hold values from 0 to 7
- rotation: bfloat16 [4, 1, 8], P(None, None, 'orb'), may hold values from -3 to 3
Outputs:
- filtered: float32 [8, 16, 48, 128], P('orb', None, 'dom')
- rotated: float32 [8, 16, 48, 128], P('orb', None, 'dom')
Inputs may be any that keep to these rules, and one draw needn't show every extreme that they name: Every draw has an orbital of degree 8 and one of degree 1. `owners`: panel numbers; panel q holds orbital q alone.
All inputs are finite; a program needn't handle non-finite values.
Results may differ from a plain program's by a relative error of at most 0.0003.
Values sent between devices are 32-bit elements; how exact they have to be, the bound alone decides.
No kernel may reach another device: no remote copies, remote signals or barrier semaphores. Data moves between devices by JAX's collectives and lax.ppermute only.
A program may use at most 64 MiB of HBM per device.

v0:
```python
import functools

import jax
import jax.numpy as jnp
from jax import lax
from jax.experimental import pallas as pl
from jax.experimental.pallas import tpu as pltpu
from jax.sharding import PartitionSpec as P

RADIUS = 6
MAXDEG = 8
STEPS = 4

STENCIL = (
    -5369.0 / 1800.0,
    12.0 / 7.0,
    -15.0 / 56.0,
    10.0 / 189.0,
    -1.0 / 112.0,
    2.0 / 1925.0,
    -1.0 / 16632.0,
)
FILTER_CENTER = 7.75
FILTER_HALF = 6.25
SCALE = 2.0 / FILTER_HALF
TAPS = tuple(-0.5 * SCALE * c for c in STENCIL[1:])
DIAGONAL = SCALE * (-1.5 * STENCIL[0] - FILTER_CENTER)


def xor_pairs(count, mask):
    return [(i, i ^ mask) for i in range(count)]


def shift_pairs(count, step):
    return [(i, i - step) for i in range(count) if 0 <= i - step < count]


def chain_kernel(whole, slots, n_dom, degree_ref, *refs):
    blocks = refs[: len(slots)]
    out_ref, even, odd, field = refs[len(slots) :]
    cells = blocks[0].shape[0] // 2
    window = even.shape[0] - 2 * RADIUS
    degree = degree_ref[0]
    dom = lax.axis_index("dom")
    if whole:
        starts = [(dom ^ k) * cells for k in slots]
        first, grid_low, grid_high = dom * cells, 0, window
    else:
        middle = window // 2 // cells * cells
        starts = [middle + k * cells for k in slots]
        first = middle
        grid_low = jnp.maximum(first - dom * cells, 0)
        grid_high = jnp.minimum(first + (n_dom - dom) * cells, window)

    edge = jnp.zeros((RADIUS,) + even.shape[1:], jnp.float32)
    for ref in (even, odd):
        ref[pl.ds(0, RADIUS)] = edge
        ref[pl.ds(RADIUS + window, RADIUS)] = edge
    if not whole:
        odd[...] = jnp.zeros(odd.shape, jnp.float32)
    for start, block in zip(starts, blocks):
        even[pl.ds(RADIUS + start, cells)] = block[:cells]
        field[pl.ds(start, cells)] = SCALE * block[cells:] + DIAGONAL

    def step(level, source, target):
        reach = RADIUS * (degree - level)
        low = jnp.maximum(first - reach, grid_low)
        high = jnp.minimum(first + cells + reach, grid_high)

        def body(index, carry):
            base = low + index * RADIUS
            for row in range(RADIUS):
                x = base + row
                center = source[RADIUS + x]
                total = field[x] * center
                for k in range(1, RADIUS + 1):
                    beside = source[RADIUS + x + k] + source[RADIUS + x - k]
                    beside = beside + (pltpu.roll(center, k, 1) + pltpu.roll(center, center.shape[1] - k, 1))
                    beside = beside + (pltpu.roll(center, k, 0) + pltpu.roll(center, center.shape[0] - k, 0))
                    total = total + TAPS[k - 1] * beside
                if level == 1:
                    target[RADIUS + x] = 0.5 * total
                else:
                    target[RADIUS + x] = total - target[RADIUS + x]
            return carry

        lax.fori_loop(0, (high - low) // RADIUS, body, 0)

    for level in range(1, MAXDEG + 1):
        source, target = (even, odd) if level % 2 else (odd, even)
        pl.when(level <= degree)(functools.partial(step, level, source, target))

    def finish(ref):
        out_ref[...] = ref[pl.ds(RADIUS + first, cells)]

    pl.when(degree % 2 == 0)(functools.partial(finish, even))
    pl.when(degree % 2 == 1)(functools.partial(finish, odd))


def combine_kernel(masks, owners_ref, mine_ref, theirs_ref, *refs):
    panels, outs = refs[: len(masks)], refs[len(masks) :]
    me = lax.axis_index("orb")
    for out, coefficients in zip(outs, (mine_ref, theirs_ref)):
        total = None
        for mask, panel in zip(masks, panels):
            weight = jnp.float32(0)
            for step in range(STEPS):
                weight = weight + jnp.where(owners_ref[step] == me ^ mask, coefficients[step], 0.0)
            term = weight * panel[...]
            total = term if total is None else total + term
        out[...] = total


def in_vmem(x):
    return pltpu.with_memory_space_constraint(x, pltpu.VMEM)


def per_device(orbitals, potential, degree, owners, rotation):
    _, planes, cells, width = orbitals.shape
    n_dom = lax.axis_size("dom")
    n_orb = lax.axis_size("orb")
    vmem = pl.BlockSpec(memory_space=pltpu.VMEM)
    smem = pl.BlockSpec(memory_space=pltpu.SMEM)
    f32 = jnp.float32
    slab = pltpu.VMEM((cells, planes, width), f32)

    orbital = jnp.transpose(orbitals[0], (1, 0, 2)).astype(f32)
    packed = jnp.concatenate([orbital, jnp.transpose(potential, (1, 0, 2))], 0)

    halo = -(-RADIUS * MAXDEG // cells)
    whole = n_dom <= 2 * halo + 1
    if whole:
        slots = list(range(n_dom))
        blocks = [packed] + [lax.ppermute(packed, "dom", xor_pairs(n_dom, k)) for k in slots[1:]]
        window = n_dom * cells
    else:
        slots = [0] + [s * k for k in range(1, halo + 1) for s in (1, -1)]
        blocks = [packed] + [lax.ppermute(packed, "dom", shift_pairs(n_dom, k)) for k in slots[1:]]
        window = (2 * halo + 1) * cells
    buffer = pltpu.VMEM((window + 2 * RADIUS, planes, width), f32)
    panel = pl.pallas_call(
        functools.partial(chain_kernel, whole, slots, n_dom),
        out_shape=slab,
        in_specs=[smem] + [vmem] * len(slots),
        out_specs=vmem,
        scratch_shapes=[buffer, buffer, pltpu.VMEM((window, planes, width), f32)],
    )(degree, *[in_vmem(b) for b in blocks])

    coefficients = rotation[:, 0, 0].astype(f32)
    beside = lax.ppermute(coefficients, "orb", xor_pairs(n_orb, 1))
    masks = sorted(range(2, n_orb, 2), key=lambda m: -m)
    panels = [panel] + [lax.ppermute(panel, "orb", xor_pairs(n_orb, m)) for m in masks]
    mine, theirs = pl.pallas_call(
        functools.partial(combine_kernel, [0] + masks),
        out_shape=(slab, slab),
        in_specs=[smem] * 3 + [vmem] * len(panels),
        out_specs=(vmem, vmem),
    )(owners, coefficients, beside, *[in_vmem(p) for p in panels])
    rotated = mine + lax.ppermute(theirs, "orb", xor_pairs(n_orb, 1))
    return tuple(jnp.transpose(x, (1, 0, 2))[None] for x in (panel, rotated))


def solution(mesh):
    placed = (
        P("orb", None, "dom", None),
        P(None, "dom", None),
        P("orb"),
        P(),
        P(None, None, "orb"),
    )
    return jax.shard_map(
        per_device,
        mesh=mesh,
        in_specs=placed,
        out_specs=(P("orb", None, "dom", None), P("orb", None, "dom", None)),
        check_vma=False,
    )
```

profile of v0, /device:TPU:0, one launch (start us, length us, event | category | flops | bytes accessed | tf_op | source)
XLA Modules:
  0.0 37.4 jit_solution(12781815360489927839)
XLA Ops:
  0.6 0.0 copy-start
  0.6 0.8 %convert_bitcast_fusion = f32[12,16,128]{2,1,0:T(8,128)S(1)} fusion(bf16[1,16,12,128]{3,1,2,0:T(8,128)(2,1)} %param.5), kind=kLoop, calls=%fused_computation.1 | loop fusion | flops 24576 | bytes 147456 | tf_op jit(solution)/shard_map/convert_element_type | solution.py:127
  1.5 0.1 copy-done
  1.6 3.0 %collective-permute-start = (f32[24,16,128]{2,1,0:T(8,128)S(1)}, f32[24,16,128]{2,1,0:T(8,128)S(1)}, u32[]{:S(2)}, u32[]{:S(2)}) collective-permute-start(f32[24,16,128]{2,1,0:T(8,128)S(1)} %pad_maximum_fusion.refs_0_), channel_id=1, source_target_pairs={{0,1},{1,0},{2,3},{3,2},{4,5},{5,4},{6,7},{7,6},{8,9},{9,8},{10,11... | collective-permute-start | bytes 589832 | tf_op jit(solution)/shard_map/ppermute | solution.py:134
  4.6 1.5 %collective-permute-start.1 = (f32[24,16,128]{2,1,0:T(8,128)S(1)}, f32[24,16,128]{2,1,0:T(8,128)S(1)}, u32[]{:S(2)}, u32[]{:S(2)}) collective-permute-start(f32[24,16,128]{2,1,0:T(8,128)S(1)} %pad_maximum_fusion.refs_0_), channel_id=1, source_target_pairs={{0,2},{1,3},{2,0},{3,1},{4,6},{5,7},{6,4},{7,5},{8,10},{9,11},{10,... | collective-permute-start | bytes 589832 | tf_op jit(solution)/shard_map/ppermute | solution.py:134
  6.1 0.0 collective-permute-start.2
  6.8 0.0 copy-start.3
  6.8 3.5 %collective-permute-done.refs_1_ = f32[24,16,128]{2,1,0:T(8,128)S(1)} collective-permute-done((f32[24,16,128]{2,1,0:T(8,128)S(1)}, f32[24,16,128]{2,1,0:T(8,128)S(1)}, u32[]{:S(2)}, u32[]{:S(2)}) %collective-permute-start) | collective-permute-done | bytes 196640 | tf_op jit(solution)/shard_map/ppermute | solution.py:134
  10.3 4.8 %collective-permute-done.1.refs_2_ = f32[24,16,128]{2,1,0:T(8,128)S(1)} collective-permute-done((f32[24,16,128]{2,1,0:T(8,128)S(1)}, f32[24,16,128]{2,1,0:T(8,128)S(1)}, u32[]{:S(2)}, u32[]{:S(2)}) %collective-permute-start.1) | collective-permute-done | bytes 196640 | tf_op jit(solution)/shard_map/ppermute | solution.py:134
  15.1 0.0 collective-permute-done.2.refs_3_
  15.1 8.1 %shard_map.68.refs_0_ = f32[12,16,128]{2,1,0:T(8,128)S(1)} custom-call(s32[1]{0:T(128)S(6)} %copy.8.degree_ref, f32[24,16,128]{2,1,0:T(8,128)S(1)} %pad_maximum_fusion.refs_0_, f32[24,16,128]{2,1,0:T(8,128)S(1)} %collective-permute-done.refs_1_, f32[24,16,128]{2,1,0:T(8,128)S(1)} %collective-permute-done.1.refs_2_, ...), custom_call_target="tpu_custom_call" | custom-call | tf_op jit(solution)/shard_map/pallas_call | solution.py:141
  23.3 1.8 %collective-permute-start.4 = (f32[12,16,128]{2,1,0:T(8,128)S(1)}, f32[12,16,128]{2,1,0:T(8,128)S(1)}, u32[]{:S(2)}, u32[]{:S(2)}) collective-permute-start(f32[12,16,128]{2,1,0:T(8,128)S(1)} %shard_map.68.refs_0_), channel_id=1, source_target_pairs={{0,24},{4,28},{8,16},{12,20},{16,8},{20,12},{24,0},{28,4},{1,25},{... | collective-permute-start | bytes 294920 | tf_op jit(solution)/shard_map/ppermute | solution.py:152
  25.1 0.0 collective-permute-start.5
  25.1 2.6 %collective-permute-start.6 = (f32[12,16,128]{2,1,0:T(8,128)S(1)}, f32[12,16,128]{2,1,0:T(8,128)S(1)}, u32[]{:S(2)}, u32[]{:S(2)}) collective-permute-start(f32[12,16,128]{2,1,0:T(8,128)S(1)} %shard_map.68.refs_0_), channel_id=1, source_target_pairs={{0,8},{4,12},{8,0},{12,4},{16,24},{20,28},{24,16},{28,20},{1,9},{5... | collective-permute-start | bytes 294920 | tf_op jit(solution)/shard_map/ppermute | solution.py:152
  27.7 0.0 copy-done.3
  27.7 0.0 copy-start.1
  27.7 0.0 collective-permute-start.3
  27.7 1.1 %collective-permute-done.3.theirs_ref = f32[4]{0:T(128)S(1)} collective-permute-done((f32[4]{0:T(128)S(1)}, f32[4]{0:T(128)S(1)}, u32[]{:S(2)}, u32[]{:S(2)}) %collective-permute-start.3) | collective-permute-done | bytes 48 | tf_op jit(solution)/shard_map/ppermute | solution.py:150
  28.9 0.0 copy-start.2
  28.9 2.0 %collective-permute-done.4.refs_1_ = f32[12,16,128]{2,1,0:T(8,128)S(1)} collective-permute-done((f32[12,16,128]{2,1,0:T(8,128)S(1)}, f32[12,16,128]{2,1,0:T(8,128)S(1)}, u32[]{:S(2)}, u32[]{:S(2)}) %collective-permute-start.4) | collective-permute-done | bytes 98336 | tf_op jit(solution)/shard_map/ppermute | solution.py:152
  30.8 3.8 %collective-permute-done.5.refs_2_ = f32[12,16,128]{2,1,0:T(8,128)S(1)} collective-permute-done((f32[12,16,128]{2,1,0:T(8,128)S(1)}, f32[12,16,128]{2,1,0:T(8,128)S(1)}, u32[]{:S(2)}, u32[]{:S(2)}) %collective-permute-start.5) | collective-permute-done | bytes 98336 | tf_op jit(solution)/shard_map/ppermute | solution.py:152
  34.6 0.0 collective-permute-done.6.refs_3_
  34.6 0.0 copy-done.1
  34.6 0.0 copy-done.2
  34.6 0.8 %shard_map.69 = (f32[12,16,128]{2,1,0:T(8,128)S(1)}, f32[12,16,128]{2,1,0:T(8,128)S(1)}) custom-call(s32[4]{0:T(128)} %owners_ref.1, f32[4]{0:T(128)} %copy-done.1, f32[4]{0:T(128)} %copy-done.2, f32[12,16,128]{2,1,0:T(8,128)S(1)} %shard_map.68.refs_0_, f32[12,16,128]{2,1,0:T(8,128)S(1)} %collective-permute-done.4.refs_1_, ...), custom_call_target="tpu_custom_call" | custom-call | tf_op jit(solution)/shard_map/pallas_call | solution.py:153
  35.4 0.1 collective-permute-start.7
  35.5 0.6 %copy.7 = f32[1,16,12,128]{3,1,2,0:T(8,128)} copy(f32[1,16,12,128]{3,1,2,0:T(8,128)S(1)} %bitcast.16) | data formatting | bytes 196608
  36.1 0.6 %collective-permute-done.7 = f32[12,16,128]{2,1,0:T(8,128)S(1)} collective-permute-done((f32[12,16,128]{2,1,0:T(8,128)S(1)}, f32[12,16,128]{2,1,0:T(8,128)S(1)}, u32[]{:S(2)}, u32[]{:S(2)}) %collective-permute-start.7) | collective-permute-done | bytes 98336 | tf_op jit(solution)/shard_map/ppermute | solution.py:159
  36.8 0.7 %add_bitcast_fusion = f32[1,16,12,128]{3,1,2,0:T(8,128)} fusion(f32[12,16,128]{2,1,0:T(8,128)S(1)} %get-tuple-element.4, f32[12,16,128]{2,1,0:T(8,128)S(1)} %collective-permute-done.7), kind=kLoop, calls=%fused_computation.2 | loop fusion | flops 24576 | bytes 294912 | tf_op jit(solution)/shard_map/broadcast_in_dim | solution.py:160
  (2 shorter events, 0.0 us)
Async XLA Ops:
  0.6 0.9 %copy-start = (f32[16,12,128]{2,0,1:T(8,128)S(1)}, f32[16,12,128]{2,0,1:T(8,128)}, u32[]{:S(2)}) copy-start(f32[16,12,128]{2,0,1:T(8,128)} %param.6) | copy-start | bytes 294916
  1.6 8.7 %collective-permute-start = (f32[24,16,128]{2,1,0:T(8,128)S(1)}, f32[24,16,128]{2,1,0:T(8,128)S(1)}, u32[]{:S(2)}, u32[]{:S(2)}) collective-permute-start(f32[24,16,128]{2,1,0:T(8,128)S(1)} %pad_maximum_fusion.refs_0_), channel_id=1, source_target_pairs={{0,1},{1,0},{2,3},{3,2},{4,5},{5,4},{6,7},{7,6},{8,9},{9,8},{10,11... | collective-permute-start | bytes 589832 | tf_op jit(solution)/shard_map/ppermute | solution.py:134
  4.6 10.6 %collective-permute-start.1 = (f32[24,16,128]{2,1,0:T(8,128)S(1)}, f32[24,16,128]{2,1,0:T(8,128)S(1)}, u32[]{:S(2)}, u32[]{:S(2)}) collective-permute-start(f32[24,16,128]{2,1,0:T(8,128)S(1)} %pad_maximum_fusion.refs_0_), channel_id=1, source_target_pairs={{0,2},{1,3},{2,0},{3,1},{4,6},{5,7},{6,4},{7,5},{8,10},{9,11},{10,... | collective-permute-start | bytes 589832 | tf_op jit(solution)/shard_map/ppermute | solution.py:134
  6.1 9.1 %collective-permute-start.2 = (f32[24,16,128]{2,1,0:T(8,128)S(1)}, f32[24,16,128]{2,1,0:T(8,128)S(1)}, u32[]{:S(2)}, u32[]{:S(2)}) collective-permute-start(f32[24,16,128]{2,1,0:T(8,128)S(1)} %pad_maximum_fusion.refs_0_), channel_id=1, source_target_pairs={{0,3},{1,2},{2,1},{3,0},{4,7},{5,6},{6,5},{7,4},{8,11},{9,10},{10,... | collective-permute-start | bytes 589832 | tf_op jit(solution)/shard_map/ppermute | solution.py:134
  6.8 21.0 %copy-start.3 = (bf16[4,1,1]{0,2,1:T(2,128)(2,1)S(1)}, bf16[4,1,1]{0,2,1:T(2,128)(2,1)}, u32[]{:S(2)}) copy-start(bf16[4,1,1]{0,2,1:T(2,128)(2,1)} %param.9) | copy-start | bytes 28
  23.3 7.6 %collective-permute-start.4 = (f32[12,16,128]{2,1,0:T(8,128)S(1)}, f32[12,16,128]{2,1,0:T(8,128)S(1)}, u32[]{:S(2)}, u32[]{:S(2)}) collective-permute-start(f32[12,16,128]{2,1,0:T(8,128)S(1)} %shard_map.68.refs_0_), channel_id=1, source_target_pairs={{0,24},{4,28},{8,16},{12,20},{16,8},{20,12},{24,0},{28,4},{1,25},{... | collective-permute-start | bytes 294920 | tf_op jit(solution)/shard_map/ppermute | solution.py:152
  25.1 9.5 %collective-permute-start.5 = (f32[12,16,128]{2,1,0:T(8,128)S(1)}, f32[12,16,128]{2,1,0:T(8,128)S(1)}, u32[]{:S(2)}, u32[]{:S(2)}) collective-permute-start(f32[12,16,128]{2,1,0:T(8,128)S(1)} %shard_map.68.refs_0_), channel_id=1, source_target_pairs={{0,16},{4,20},{8,24},{12,28},{16,0},{20,4},{24,8},{28,12},{1,17},{... | collective-permute-start | bytes 294920 | tf_op jit(solution)/shard_map/ppermute | solution.py:152
  25.1 9.5 %collective-permute-start.6 = (f32[12,16,128]{2,1,0:T(8,128)S(1)}, f32[12,16,128]{2,1,0:T(8,128)S(1)}, u32[]{:S(2)}, u32[]{:S(2)}) collective-permute-start(f32[12,16,128]{2,1,0:T(8,128)S(1)} %shard_map.68.refs_0_), channel_id=1, source_target_pairs={{0,8},{4,12},{8,0},{12,4},{16,24},{20,28},{24,16},{28,20},{1,9},{5... | collective-permute-start | bytes 294920 | tf_op jit(solution)/shard_map/ppermute | solution.py:152
  27.7 6.9 %copy-start.1 = (f32[4]{0:T(128)}, f32[4]{0:T(128)S(1)}, u32[]{:S(2)}) copy-start(f32[4]{0:T(128)S(1)} %bitcast_convert_fusion.mine_ref) | copy-start | bytes 52
  27.7 1.1 %collective-permute-start.3 = (f32[4]{0:T(128)S(1)}, f32[4]{0:T(128)S(1)}, u32[]{:S(2)}, u32[]{:S(2)}) collective-permute-start(f32[4]{0:T(128)S(1)} %bitcast_convert_fusion.mine_ref), channel_id=1, source_target_pairs={{0,4},{4,0},{8,12},{12,8},{16,20},{20,16},{24,28},{28,24},{1,5},{5... | collective-permute-start | bytes 56 | tf_op jit(solution)/shard_map/ppermute | solution.py:150
  28.9 5.8 %copy-start.2 = (f32[4]{0:T(128)}, f32[4]{0:T(128)S(1)}, u32[]{:S(2)}) copy-start(f32[4]{0:T(128)S(1)} %collective-permute-done.3.theirs_ref) | copy-start | bytes 52
  35.4 1.4 %collective-permute-start.7 = (f32[12,16,128]{2,1,0:T(8,128)S(1)}, f32[12,16,128]{2,1,0:T(8,128)S(1)}, u32[]{:S(2)}, u32[]{:S(2)}) collective-permute-start(f32[12,16,128]{2,1,0:T(8,128)S(1)} %get-tuple-element.5), channel_id=1, source_target_pairs={{0,4},{4,0},{8,12},{12,8},{16,20},{20,16},{24,28},{28,24},{1,5},{5... | collective-permute-start | bytes 294920 | tf_op jit(solution)/shard_map/ppermute | solution.py:159
where the time goes:
time: 38.1 us; the launch traced here: 37.4 us
  waiting for transfers between devices  15.9 us (42%)
  starting transfers between devices  9.11 us (24%)
  Pallas kernels  8.87 us (23%)
  other arithmetic  1.51 us (4%)
  between operations  1.34 us (4%)
  local copies, waits for them, and re-layouts  0.72 us (2%)
    ppermute x3, waiting for transfers between devices, per_device(): lax.ppermute(packed, 'dom', xor_pairs(n_dom, k))  8.37 us
    pallas_call x1, Pallas kernels, per_device(): pl.pallas_call(functools.partial(chain_kernel, whole, slots, n_dom), out_...  8.12 us
    ppermute x3, waiting for transfers between devices, per_device(): lax.ppermute(panel, 'orb', xor_pairs(n_orb, m))  5.77 us
    ppermute x3, starting transfers between devices, per_device(): lax.ppermute(packed, 'dom', xor_pairs(n_dom, k))  4.54 us
    ppermute x3, starting transfers between devices, per_device(): lax.ppermute(panel, 'orb', xor_pairs(n_orb, m))  4.45 us
    ppermute x1, waiting for transfers between devices, per_device(): beside = lax.ppermute(coefficients, 'orb', xor_pairs(n_orb, 1))  1.11 us
    convert_element_type x1, other arithmetic, per_device(): orbital = jnp.transpose(orbitals[0], (1, 0, 2)).astype(f32)  0.84 us
  transfers between devices with their start and end apart: 8, of which 6 were waited for; matrix products, arithmetic and copies ran while one was open for 2% of the time, Pallas kernels for 0%

commit v1 on v0

v1 whole, which is shorter than its diff:
```python
import functools

import jax
import jax.numpy as jnp
import ml_dtypes
import numpy as np
from jax import lax
from jax.experimental import pallas as pl
from jax.experimental.pallas import tpu as pltpu
from jax.sharding import PartitionSpec as P

RADIUS = 6
MAXDEG = 8
STEPS = 4

STENCIL = (
    -5369.0 / 1800.0,
    12.0 / 7.0,
    -15.0 / 56.0,
    10.0 / 189.0,
    -1.0 / 112.0,
    2.0 / 1925.0,
    -1.0 / 16632.0,
)
FILTER_CENTER = 7.75
FILTER_HALF = 6.25
SCALE = 2.0 / FILTER_HALF
TAPS = tuple(-0.5 * SCALE * c for c in STENCIL[1:])
DIAGONAL = SCALE * (-1.5 * STENCIL[0] - FILTER_CENTER)


def xor_pairs(count, mask):
    return [(i, i ^ mask) for i in range(count)]


def shift_pairs(count, step):
    return [(i, i - step) for i in range(count) if 0 <= i - step < count]


def split(values):
    high = values.astype(jnp.bfloat16)
    return high, (values - high.astype(jnp.float32)).astype(jnp.bfloat16)


def ring(count, copies):
    matrix = np.zeros((count, count), np.float64)
    for k, tap in enumerate(TAPS, 1):
        for i in range(count):
            matrix[i, (i + k) % count] += tap
            matrix[i, (i - k) % count] += tap
    matrix = np.kron(np.eye(copies), matrix)
    high = matrix.astype(ml_dtypes.bfloat16)
    low = (matrix - high.astype(np.float64)).astype(ml_dtypes.bfloat16)
    return high, low


def chain_kernel(whole, slots, groups, n_dom, degree_ref, rows_ref, *refs):
    planes_at = dict(zip(groups, refs))
    refs = refs[len(groups) :]
    blocks = refs[: len(slots)]
    out_ref, *fields, potential = refs[len(slots) :]
    cells = blocks[0].shape[0] // 2
    planes, width = potential.shape[1:]
    window = potential.shape[0]
    n_blocks = window // cells
    degree = degree_ref[0]
    dom = lax.axis_index("dom")
    home = dom if whole else n_blocks // 2
    starts = [(dom ^ k if whole else home + k) * cells for k in slots]
    rows = cells * planes

    for start, block in zip(starts, blocks):
        potential[pl.ds(start, cells)] = SCALE * block[cells:] + DIAGONAL
    for ref in fields:
        ref[pl.ds(0, RADIUS)] = jnp.zeros((RADIUS, planes, width), jnp.float32)
        ref[pl.ds(RADIUS + window, RADIUS)] = jnp.zeros((RADIUS, planes, width), jnp.float32)

    def begin(current, previous):
        for start, block in zip(starts, blocks):
            current[pl.ds(RADIUS + start, cells)] = block[:cells]
        previous[pl.ds(RADIUS, window)] = jnp.zeros((window, planes, width), jnp.float32)

    pl.when(degree % 2 == 0)(functools.partial(begin, fields[0], fields[1]))
    pl.when(degree % 2 == 1)(functools.partial(begin, fields[1], fields[0]))

    def advance(parity, factor, start, count):
        source, target = fields[1 - parity], fields[parity]
        base = start * cells
        high, low = split(source[pl.ds(RADIUS + base, count * cells)].reshape(count * rows, width))
        both = jnp.concatenate([high, low], 1)
        across = jnp.dot(both, rows_ref[...], preferred_element_type=jnp.float32)
        group = max(m for m in planes_at if count * cells % (2 * m) == 0)
        size = group * planes
        alongs = []
        for top in range(0, count * rows, 2 * size):
            pieces = [jnp.concatenate([v[top : top + size], v[top + size : top + 2 * size]], 1) for v in (high, low)]
            alongs.append(
                jnp.dot(
                    planes_at[group][...], jnp.concatenate(pieces, 0), preferred_element_type=jnp.float32
                )
            )
        for part in range(0, count * cells, RADIUS):
            x = base + part
            near = source[pl.ds(x, 3 * RADIUS)]
            total = potential[pl.ds(x, RADIUS)] * near[RADIUS : 2 * RADIUS]
            for k in range(1, RADIUS + 1):
                beside = near[RADIUS + k : 2 * RADIUS + k] + near[RADIUS - k : 2 * RADIUS - k]
                total = total + TAPS[k - 1] * beside
            spot = pl.ds(RADIUS + x, RADIUS)
            target[spot] = factor * total - target[spot]
        for index, along in enumerate(alongs):
            along = along[:size] + along[size:]
            for half in range(2):
                top = (2 * index + half) * size
                plane_sum = across[top : top + size, :width] + across[top : top + size, width:]
                plane_sum = plane_sum + along[:, half * width : (half + 1) * width]
                spot = pl.ds(RADIUS + base + (2 * index + half) * group, group)
                target[spot] = target[spot] + factor * plane_sum.reshape(group, planes, width)

    def level(left, parity, reach):
        count = min(2 * reach + 1, n_blocks)
        factor = jnp.where(left == degree - 1, 0.5, 1.0)
        if whole:
            advance(parity, factor, jnp.clip(home - reach, 0, n_blocks - count), count)
            return
        for block in range(home - reach, home - reach + count):
            place = dom + block - home
            pl.when((place >= 0) & (place < n_dom))(functools.partial(advance, parity, factor, block, 1))

    def levels(fewest, most, reach):
        top = jnp.minimum(most, degree - 1)
        parity = fewest % 2

        def pair(index, carry):
            left = fewest + 2 * (count // 2 - index) - 1
            level(left, 1 - parity, reach)
            level(left - 1, parity, reach)
            return carry

        count = jnp.maximum(top - fewest + 1, 0)
        if most > fewest:
            pl.when(count % 2 == 1)(lambda: level(top, parity, reach))
            lax.fori_loop(0, count // 2, pair, 0)
        else:
            pl.when(count == 1)(lambda: level(fewest, parity, reach))

    bounds = [-(-RADIUS * left // cells) for left in range(MAXDEG)]
    if whole:
        bounds = [min(reach, n_blocks // 2) for reach in bounds]
    for reach in sorted(set(bounds), reverse=True):
        lefts = [left for left in range(MAXDEG) if bounds[left] == reach]
        levels(lefts[0], lefts[-1], reach)
    out_ref[...] = fields[0][pl.ds(RADIUS + home * cells, cells)]


def combine_kernel(masks, owners_ref, mine_ref, theirs_ref, *refs):
    panels, outs = refs[: len(masks)], refs[len(masks) :]
    me = lax.axis_index("orb")
    for out, coefficients in zip(outs, (mine_ref, theirs_ref)):
        total = None
        for mask, panel in zip(masks, panels):
            weight = jnp.float32(0)
            for step in range(STEPS):
                weight = weight + jnp.where(owners_ref[step] == me ^ mask, coefficients[step], 0.0)
            term = weight * panel[...]
            total = term if total is None else total + term
        out[...] = total


def in_vmem(x):
    return pltpu.with_memory_space_constraint(x, pltpu.VMEM)


def chain(degree, blocks, n_dom):
    cells, planes, width = blocks[0].shape[0] // 2, *blocks[0].shape[1:]
    halo = -(-RADIUS * MAXDEG // cells)
    whole = n_dom <= 2 * halo + 1
    if whole:
        slots = list(range(n_dom))
        window = n_dom * cells
        counts = range(1, n_dom + 1)
    else:
        slots = [0] + [s * k for k in range(1, halo + 1) for s in (1, -1)]
        window = (2 * halo + 1) * cells
        counts = [1]
    high, low = ring(width, 1)
    across = np.block([[high, low], [high, low]])
    groups = sorted({max(g for g in range(1, width // planes + 1) if c * cells % (2 * g) == 0) for c in counts})
    alongs = [np.block([[m, m] for m in ring(planes, g)]) for g in groups]
    field = pltpu.VMEM((window + 2 * RADIUS, planes, width), jnp.float32)
    vmem = pl.BlockSpec(memory_space=pltpu.VMEM)
    smem = pl.BlockSpec(memory_space=pltpu.SMEM)
    return pl.pallas_call(
        functools.partial(chain_kernel, whole, slots, groups, n_dom),
        out_shape=pltpu.VMEM((cells, planes, width), jnp.float32),
        in_specs=[smem] + [vmem] * (1 + len(groups) + len(slots)),
        out_specs=vmem,
        scratch_shapes=[field, field, pltpu.VMEM((window, planes, width), jnp.float32)],
    )(degree, *[in_vmem(b) for b in [jnp.asarray(m) for m in [across] + alongs] + blocks])


def per_device(orbitals, potential, degree, owners, rotation):
    _, planes, cells, width = orbitals.shape
    n_dom = lax.axis_size("dom")
    n_orb = lax.axis_size("orb")
    vmem = pl.BlockSpec(memory_space=pltpu.VMEM)
    smem = pl.BlockSpec(memory_space=pltpu.SMEM)
    f32 = jnp.float32
    slab = pltpu.VMEM((cells, planes, width), f32)

    orbital = jnp.transpose(orbitals[0], (1, 0, 2)).astype(f32)
    packed = jnp.concatenate([orbital, jnp.transpose(potential, (1, 0, 2))], 0)

    halo = -(-RADIUS * MAXDEG // cells)
    if n_dom <= 2 * halo + 1:
        pairs = [xor_pairs(n_dom, k) for k in range(1, n_dom)]
    else:
        pairs = [shift_pairs(n_dom, s * k) for k in range(1, halo + 1) for s in (1, -1)]
    panel = chain(degree, [packed] + [lax.ppermute(packed, "dom", p) for p in pairs], n_dom)

    coefficients = rotation[:, 0, 0].astype(f32)
    beside = lax.ppermute(coefficients, "orb", xor_pairs(n_orb, 1))
    masks = sorted(range(2, n_orb, 2), key=lambda m: -m)
    panels = [panel] + [lax.ppermute(panel, "orb", xor_pairs(n_orb, m)) for m in masks]
    mine, theirs = pl.pallas_call(
        functools.partial(combine_kernel, [0] + masks),
        out_shape=(slab, slab),
        in_specs=[smem] * 3 + [vmem] * len(panels),
        out_specs=(vmem, vmem),
    )(owners, coefficients, beside, *[in_vmem(p) for p in panels])
    rotated = mine + lax.ppermute(theirs, "orb", xor_pairs(n_orb, 1))
    return tuple(jnp.transpose(x, (1, 0, 2))[None] for x in (panel, rotated))


def solution(mesh):
    placed = (
        P("orb", None, "dom", None),
        P(None, "dom", None),
        P("orb"),
        P(),
        P(None, None, "orb"),
    )
    return jax.shard_map(
        per_device,
        mesh=mesh,
        in_specs=placed,
        out_specs=(P("orb", None, "dom", None), P("orb", None, "dom", None)),
        check_vma=False,
    )
```

time: 38.1 us -> 32.3 us (0.85); the launches traced: 37.4 us -> 32.1 us
  Pallas kernels: 8.87 us -> 1.13 us
  starting transfers between devices: 9.11 us -> 12.1 us
  waiting for transfers between devices: 15.9 us -> 15.3 us
    pallas_call x1, Pallas kernels: 8.12 us -> 0.38 us  [chain(): pl.pallas_call(functools.partial(chain_kernel, whole, slots, groups, n_do...]
    ppermute x3, starting transfers between devices: 4.45 us -> 7.47 us  [per_device(): lax.ppermute(panel, 'orb', xor_pairs(n_orb, m))]
    ppermute x3, waiting for transfers between devices: 5.77 us -> 5.19 us  [per_device(): lax.ppermute(panel, 'orb', xor_pairs(n_orb, m))]
where the time goes in v1:
time: 32.3 us; the launch traced here: 32.1 us
  waiting for transfers between devices  15.3 us (47%)
  starting transfers between devices  12.1 us (37%)
  other arithmetic  1.51 us (5%)
  between operations  1.36 us (4%)
  Pallas kernels  1.13 us (3%)
  local copies, waits for them, and re-layouts  0.74 us (2%)
    ppermute x3, waiting for transfers between devices, per_device(): lax.ppermute(packed, 'dom', p)  8.37 us
    ppermute x3, starting transfers between devices, per_device(): lax.ppermute(panel, 'orb', xor_pairs(n_orb, m))  7.47 us
    ppermute x3, waiting for transfers between devices, per_device(): lax.ppermute(panel, 'orb', xor_pairs(n_orb, m))  5.19 us
    ppermute x3, starting transfers between devices, per_device(): lax.ppermute(packed, 'dom', p)  4.54 us
    ppermute x1, waiting for transfers between devices, per_device(): beside = lax.ppermute(coefficients, 'orb', xor_pairs(n_orb, 1))  1.11 us
    convert_element_type x1, other arithmetic, per_device(): orbital = jnp.transpose(orbitals[0], (1, 0, 2)).astype(f32)  0.84 us
    pallas_call x1, Pallas kernels, per_device(): pl.pallas_call(functools.partial(combine_kernel, [0] + masks), out_shape=...  0.75 us
    unnamed x15, local copies, waits for them, and re-layouts  0.74 us
  transfers between devices with their start and end apart: 8, of which 6 were waited for; matrix products, arithmetic and copies ran while one was open for 2% of the time, Pallas kernels for 0%

profile of v1, /device:TPU:0, one launch (start us, length us, event | category | flops | bytes accessed | tf_op | source)
XLA Modules:
  0.0 32.1 jit_solution(5406023141694566425)
XLA Ops:
  0.6 0.0 copy-start.3
  0.6 0.8 %convert_bitcast_fusion = f32[12,16,128]{2,1,0:T(8,128)S(1)} fusion(bf16[1,16,12,128]{3,1,2,0:T(8,128)(2,1)} %param.8), kind=kLoop, calls=%fused_computation.1 | loop fusion | flops 24576 | bytes 147456 | tf_op jit(solution)/shard_map/convert_element_type | solution.py:211
  1.5 0.1 copy-done.3
  1.5 0.0 copy-start
  1.5 0.0 copy-start.1
  1.6 0.0 copy-start.2
  1.6 3.0 %collective-permute-start = (f32[24,16,128]{2,1,0:T(8,128)S(1)}, f32[24,16,128]{2,1,0:T(8,128)S(1)}, u32[]{:S(2)}, u32[]{:S(2)}) collective-permute-start(f32[24,16,128]{2,1,0:T(8,128)S(1)} %pad_maximum_fusion.refs_2_), channel_id=1, source_target_pairs={{0,1},{1,0},{2,3},{3,2},{4,5},{5,4},{6,7},{7,6},{8,9},{9,8},{10,11... | collective-permute-start | bytes 589832 | tf_op jit(solution)/shard_map/ppermute | solution.py:219
  4.6 1.5 %collective-permute-start.1 = (f32[24,16,128]{2,1,0:T(8,128)S(1)}, f32[24,16,128]{2,1,0:T(8,128)S(1)}, u32[]{:S(2)}, u32[]{:S(2)}) collective-permute-start(f32[24,16,128]{2,1,0:T(8,128)S(1)} %pad_maximum_fusion.refs_2_), channel_id=1, source_target_pairs={{0,2},{1,3},{2,0},{3,1},{4,6},{5,7},{6,4},{7,5},{8,10},{9,11},{10,... | collective-permute-start | bytes 589832 | tf_op jit(solution)/shard_map/ppermute | solution.py:219
  6.1 0.0 collective-permute-start.2
  6.8 0.0 copy-start.6
  6.8 3.5 %collective-permute-done.refs_3_ = f32[24,16,128]{2,1,0:T(8,128)S(1)} collective-permute-done((f32[24,16,128]{2,1,0:T(8,128)S(1)}, f32[24,16,128]{2,1,0:T(8,128)S(1)}, u32[]{:S(2)}, u32[]{:S(2)}) %collective-permute-start) | collective-permute-done | bytes 196640 | tf_op jit(solution)/shard_map/ppermute | solution.py:219
  10.3 4.8 %collective-permute-done.1.refs_4_ = f32[24,16,128]{2,1,0:T(8,128)S(1)} collective-permute-done((f32[24,16,128]{2,1,0:T(8,128)S(1)}, f32[24,16,128]{2,1,0:T(8,128)S(1)}, u32[]{:S(2)}, u32[]{:S(2)}) %collective-permute-start.1) | collective-permute-done | bytes 196640 | tf_op jit(solution)/shard_map/ppermute | solution.py:219
  15.1 0.0 collective-permute-done.2.refs_5_
  15.2 0.0 copy-done
  15.2 0.0 copy-done.1
  15.2 0.0 copy-done.2
  15.2 0.4 %shard_map.95.refs_0_ = f32[12,16,128]{2,1,0:T(8,128)S(1)} custom-call(s32[1]{0:T(128)S(6)} %copy.11.degree_ref, bf16[256,256]{1,0:T(8,128)(2,1)S(1)} %copy-done, bf16[192,192]{1,0:T(8,128)(2,1)S(1)} %copy-done.2, bf16[256,256]{1,0:T(8,128)(2,1)S(1)} %copy-done.1, f32[24,16,128]{2,1,0:T(8,128)S(1)} %pad_maximum_fusion.refs_2_, ...), custom_call_target="tpu_custom_call" | custom-call | tf_op jit(solution)/shard_map/pallas_call | solution.py:193
  15.6 6.8 %collective-permute-start.4 = (f32[12,16,128]{2,1,0:T(8,128)S(1)}, f32[12,16,128]{2,1,0:T(8,128)S(1)}, u32[]{:S(2)}, u32[]{:S(2)}) collective-permute-start(f32[12,16,128]{2,1,0:T(8,128)S(1)} %shard_map.95.refs_0_), channel_id=1, source_target_pairs={{0,24},{4,28},{8,16},{12,20},{16,8},{20,12},{24,0},{28,4},{1,25},{... | collective-permute-start | bytes 294920 | tf_op jit(solution)/shard_map/ppermute | solution.py:224
  22.4 0.0 collective-permute-start.5
  22.4 0.6 %collective-permute-start.6 = (f32[12,16,128]{2,1,0:T(8,128)S(1)}, f32[12,16,128]{2,1,0:T(8,128)S(1)}, u32[]{:S(2)}, u32[]{:S(2)}) collective-permute-start(f32[12,16,128]{2,1,0:T(8,128)S(1)} %shard_map.95.refs_0_), channel_id=1, source_target_pairs={{0,8},{4,12},{8,0},{12,4},{16,24},{20,28},{24,16},{28,20},{1,9},{5... | collective-permute-start | bytes 294920 | tf_op jit(solution)/shard_map/ppermute | solution.py:224
  23.0 0.0 copy-done.6
  23.0 0.0 copy-start.4
  23.0 0.0 collective-permute-start.3
  23.0 1.1 %collective-permute-done.3.theirs_ref = f32[4]{0:T(128)S(1)} collective-permute-done((f32[4]{0:T(128)S(1)}, f32[4]{0:T(128)S(1)}, u32[]{:S(2)}, u32[]{:S(2)}) %collective-permute-start.3) | collective-permute-done | bytes 48 | tf_op jit(solution)/shard_map/ppermute | solution.py:222
  24.1 0.0 copy-start.5
  24.2 1.3 %collective-permute-done.4.refs_1_ = f32[12,16,128]{2,1,0:T(8,128)S(1)} collective-permute-done((f32[12,16,128]{2,1,0:T(8,128)S(1)}, f32[12,16,128]{2,1,0:T(8,128)S(1)}, u32[]{:S(2)}, u32[]{:S(2)}) %collective-permute-start.4) | collective-permute-done | bytes 98336 | tf_op jit(solution)/shard_map/ppermute | solution.py:224
  25.5 3.9 %collective-permute-done.5.refs_2_ = f32[12,16,128]{2,1,0:T(8,128)S(1)} collective-permute-done((f32[12,16,128]{2,1,0:T(8,128)S(1)}, f32[12,16,128]{2,1,0:T(8,128)S(1)}, u32[]{:S(2)}, u32[]{:S(2)}) %collective-permute-start.5) | collective-permute-done | bytes 98336 | tf_op jit(solution)/shard_map/ppermute | solution.py:224
  29.3 0.0 collective-permute-done.6.refs_3_
  29.3 0.0 copy-done.4
  29.4 0.0 copy-done.5
  29.4 0.8 %shard_map.96 = (f32[12,16,128]{2,1,0:T(8,128)S(1)}, f32[12,16,128]{2,1,0:T(8,128)S(1)}) custom-call(s32[4]{0:T(128)} %owners_ref.1, f32[4]{0:T(128)} %copy-done.4, f32[4]{0:T(128)} %copy-done.5, f32[12,16,128]{2,1,0:T(8,128)S(1)} %shard_map.95.refs_0_, f32[12,16,128]{2,1,0:T(8,128)S(1)} %collective-permute-done.4.refs_1_, ...), custom_call_target="tpu_custom_call" | custom-call | tf_op jit(solution)/shard_map/pallas_call | solution.py:225
  30.1 0.1 collective-permute-start.7
  30.2 0.6 %copy.10 = f32[1,16,12,128]{3,1,2,0:T(8,128)} copy(f32[1,16,12,128]{3,1,2,0:T(8,128)S(1)} %bitcast.16) | data formatting | bytes 196608
  30.8 0.6 %collective-permute-done.7 = f32[12,16,128]{2,1,0:T(8,128)S(1)} collective-permute-done((f32[12,16,128]{2,1,0:T(8,128)S(1)}, f32[12,16,128]{2,1,0:T(8,128)S(1)}, u32[]{:S(2)}, u32[]{:S(2)}) %collective-permute-start.7) | collective-permute-done | bytes 98336 | tf_op jit(solution)/shard_map/ppermute | solution.py:231
  31.5 0.7 %add_bitcast_fusion = f32[1,16,12,128]{3,1,2,0:T(8,128)} fusion(f32[12,16,128]{2,1,0:T(8,128)S(1)} %get-tuple-element.4, f32[12,16,128]{2,1,0:T(8,128)S(1)} %collective-permute-done.7), kind=kLoop, calls=%fused_computation.2 | loop fusion | flops 24576 | bytes 294912 | tf_op jit(solution)/shard_map/broadcast_in_dim | solution.py:232
  (2 shorter events, 0.0 us)
Async XLA Ops:
  0.6 0.9 %copy-start.3 = (f32[16,12,128]{2,0,1:T(8,128)S(1)}, f32[16,12,128]{2,0,1:T(8,128)}, u32[]{:S(2)}) copy-start(f32[16,12,128]{2,0,1:T(8,128)} %param.9) | copy-start | bytes 294916
  1.5 13.6 %copy-start = (bf16[256,256]{1,0:T(8,128)(2,1)S(1)}, bf16[256,256]{1,0:T(8,128)(2,1)}, u32[]{:S(2)}) copy-start(bf16[256,256]{1,0:T(8,128)(2,1)} %constant.6.clone.rows_ref) | copy-start | bytes 393220
  1.5 13.6 %copy-start.1 = (bf16[256,256]{1,0:T(8,128)(2,1)S(1)}, bf16[256,256]{1,0:T(8,128)(2,1)}, u32[]{:S(2)}) copy-start(bf16[256,256]{1,0:T(8,128)(2,1)} %constant.8.clone.refs_1_) | copy-start | bytes 393220
  1.6 13.6 %copy-start.2 = (bf16[192,192]{1,0:T(8,128)(2,1)S(1)}, bf16[192,192]{1,0:T(8,128)(2,1)}, u32[]{:S(2)}) copy-start(bf16[192,192]{1,0:T(8,128)(2,1)} %constant.7.clone.refs_0_) | copy-start | bytes 221188
  1.6 8.7 %collective-permute-start = (f32[24,16,128]{2,1,0:T(8,128)S(1)}, f32[24,16,128]{2,1,0:T(8,128)S(1)}, u32[]{:S(2)}, u32[]{:S(2)}) collective-permute-start(f32[24,16,128]{2,1,0:T(8,128)S(1)} %pad_maximum_fusion.refs_2_), channel_id=1, source_target_pairs={{0,1},{1,0},{2,3},{3,2},{4,5},{5,4},{6,7},{7,6},{8,9},{9,8},{10,11... | collective-permute-start | bytes 589832 | tf_op jit(solution)/shard_map/ppermute | solution.py:219
  4.6 10.6 %collective-permute-start.1 = (f32[24,16,128]{2,1,0:T(8,128)S(1)}, f32[24,16,128]{2,1,0:T(8,128)S(1)}, u32[]{:S(2)}, u32[]{:S(2)}) collective-permute-start(f32[24,16,128]{2,1,0:T(8,128)S(1)} %pad_maximum_fusion.refs_2_), channel_id=1, source_target_pairs={{0,2},{1,3},{2,0},{3,1},{4,6},{5,7},{6,4},{7,5},{8,10},{9,11},{10,... | collective-permute-start | bytes 589832 | tf_op jit(solution)/shard_map/ppermute | solution.py:219
  6.1 9.1 %collective-permute-start.2 = (f32[24,16,128]{2,1,0:T(8,128)S(1)}, f32[24,16,128]{2,1,0:T(8,128)S(1)}, u32[]{:S(2)}, u32[]{:S(2)}) collective-permute-start(f32[24,16,128]{2,1,0:T(8,128)S(1)} %pad_maximum_fusion.refs_2_), channel_id=1, source_target_pairs={{0,3},{1,2},{2,1},{3,0},{4,7},{5,6},{6,5},{7,4},{8,11},{9,10},{10,... | collective-permute-start | bytes 589832 | tf_op jit(solution)/shard_map/ppermute | solution.py:219
  6.8 16.3 %copy-start.6 = (bf16[4,1,1]{0,2,1:T(2,128)(2,1)S(1)}, bf16[4,1,1]{0,2,1:T(2,128)(2,1)}, u32[]{:S(2)}) copy-start(bf16[4,1,1]{0,2,1:T(2,128)(2,1)} %param.12) | copy-start | bytes 28
  15.6 9.9 %collective-permute-start.4 = (f32[12,16,128]{2,1,0:T(8,128)S(1)}, f32[12,16,128]{2,1,0:T(8,128)S(1)}, u32[]{:S(2)}, u32[]{:S(2)}) collective-permute-start(f32[12,16,128]{2,1,0:T(8,128)S(1)} %shard_map.95.refs_0_), channel_id=1, source_target_pairs={{0,24},{4,28},{8,16},{12,20},{16,8},{20,12},{24,0},{28,4},{1,25},{... | collective-permute-start | bytes 294920 | tf_op jit(solution)/shard_map/ppermute | solution.py:224
  22.4 7.0 %collective-permute-start.5 = (f32[12,16,128]{2,1,0:T(8,128)S(1)}, f32[12,16,128]{2,1,0:T(8,128)S(1)}, u32[]{:S(2)}, u32[]{:S(2)}) collective-permute-start(f32[12,16,128]{2,1,0:T(8,128)S(1)} %shard_map.95.refs_0_), channel_id=1, source_target_pairs={{0,16},{4,20},{8,24},{12,28},{16,0},{20,4},{24,8},{28,12},{1,17},{... | collective-permute-start | bytes 294920 | tf_op jit(solution)/shard_map/ppermute | solution.py:224
  22.4 7.0 %collective-permute-start.6 = (f32[12,16,128]{2,1,0:T(8,128)S(1)}, f32[12,16,128]{2,1,0:T(8,128)S(1)}, u32[]{:S(2)}, u32[]{:S(2)}) collective-permute-start(f32[12,16,128]{2,1,0:T(8,128)S(1)} %shard_map.95.refs_0_), channel_id=1, source_target_pairs={{0,8},{4,12},{8,0},{12,4},{16,24},{20,28},{24,16},{28,20},{1,9},{5... | collective-permute-start | bytes 294920 | tf_op jit(solution)/shard_map/ppermute | solution.py:224
  23.0 6.3 %copy-start.4 = (f32[4]{0:T(128)}, f32[4]{0:T(128)S(1)}, u32[]{:S(2)}) copy-start(f32[4]{0:T(128)S(1)} %bitcast_convert_fusion.mine_ref) | copy-start | bytes 52
  23.0 1.1 %collective-permute-start.3 = (f32[4]{0:T(128)S(1)}, f32[4]{0:T(128)S(1)}, u32[]{:S(2)}, u32[]{:S(2)}) collective-permute-start(f32[4]{0:T(128)S(1)} %bitcast_convert_fusion.mine_ref), channel_id=1, source_target_pairs={{0,4},{4,0},{8,12},{12,8},{16,20},{20,16},{24,28},{28,24},{1,5},{5... | collective-permute-start | bytes 56 | tf_op jit(solution)/shard_map/ppermute | solution.py:222
  24.1 5.2 %copy-start.5 = (f32[4]{0:T(128)}, f32[4]{0:T(128)S(1)}, u32[]{:S(2)}) copy-start(f32[4]{0:T(128)S(1)} %collective-permute-done.3.theirs_ref) | copy-start | bytes 52
  30.1 1.4 %collective-permute-start.7 = (f32[12,16,128]{2,1,0:T(8,128)S(1)}, f32[12,16,128]{2,1,0:T(8,128)S(1)}, u32[]{:S(2)}, u32[]{:S(2)}) collective-permute-start(f32[12,16,128]{2,1,0:T(8,128)S(1)} %get-tuple-element.5), channel_id=1, source_target_pairs={{0,4},{4,0},{8,12},{12,8},{16,20},{20,16},{24,28},{28,24},{1,5},{5... | collective-permute-start | bytes 294920 | tf_op jit(solution)/shard_map/ppermute | solution.py:231

commit v2 on v1

--- a/solution.py
+++ b/solution.py
@@ -62,12 +62,10 @@
     cells = blocks[0].shape[0] // 2
     planes, width = potential.shape[1:]
     window = potential.shape[0]
-    n_blocks = window // cells
     degree = degree_ref[0]
     dom = lax.axis_index("dom")
-    home = dom if whole else n_blocks // 2
+    home = dom if whole else window // cells // 2
     starts = [(dom ^ k if whole else home + k) * cells for k in slots]
-    rows = cells * planes
 
     for start, block in zip(starts, blocks):
         potential[pl.ds(start, cells)] = SCALE * block[cells:] + DIAGONAL
@@ -83,23 +81,22 @@
     pl.when(degree % 2 == 0)(functools.partial(begin, fields[0], fields[1]))
     pl.when(degree % 2 == 1)(functools.partial(begin, fields[1], fields[0]))
 
-    def advance(parity, factor, start, count):
+    def advance(parity, factor, base, extent):
         source, target = fields[1 - parity], fields[parity]
-        base = start * cells
-        high, low = split(source[pl.ds(RADIUS + base, count * cells)].reshape(count * rows, width))
+        high, low = split(source[pl.ds(RADIUS + base, extent)].reshape(extent * planes, width))
         both = jnp.concatenate([high, low], 1)
         across = jnp.dot(both, rows_ref[...], preferred_element_type=jnp.float32)
-        group = max(m for m in planes_at if count * cells % (2 * m) == 0)
+        group = max(m for m in planes_at if extent % (2 * m) == 0)
         size = group * planes
         alongs = []
-        for top in range(0, count * rows, 2 * size):
+        for top in range(0, extent * planes, 2 * size):
             pieces = [jnp.concatenate([v[top : top + size], v[top + size : top + 2 * size]], 1) for v in (high, low)]
             alongs.append(
                 jnp.dot(
                     planes_at[group][...], jnp.concatenate(pieces, 0), preferred_element_type=jnp.float32
                 )
             )
-        for part in range(0, count * cells, RADIUS):
+        for part in range(0, extent, RADIUS):
             x = base + part
             near = source[pl.ds(x, 3 * RADIUS)]
             total = potential[pl.ds(x, RADIUS)] * near[RADIUS : 2 * RADIUS]
@@ -118,14 +115,14 @@
                 target[spot] = target[spot] + factor * plane_sum.reshape(group, planes, width)
 
     def level(left, parity, reach):
-        count = min(2 * reach + 1, n_blocks)
         factor = jnp.where(left == degree - 1, 0.5, 1.0)
         if whole:
-            advance(parity, factor, jnp.clip(home - reach, 0, n_blocks - count), count)
+            extent = min(cells + 2 * reach, window)
+            advance(parity, factor, jnp.clip(home * cells - reach, 0, window - extent), extent)
             return
-        for block in range(home - reach, home - reach + count):
+        for block in range(home - -(-reach // cells), home + -(-reach // cells) + 1):
             place = dom + block - home
-            pl.when((place >= 0) & (place < n_dom))(functools.partial(advance, parity, factor, block, 1))
+            pl.when((place >= 0) & (place < n_dom))(functools.partial(advance, parity, factor, block * cells, cells))
 
     def levels(fewest, most, reach):
         top = jnp.minimum(most, degree - 1)
@@ -144,27 +141,23 @@
         else:
             pl.when(count == 1)(lambda: level(fewest, parity, reach))
 
-    bounds = [-(-RADIUS * left // cells) for left in range(MAXDEG)]
+    bounds = [RADIUS * left for left in range(MAXDEG)]
     if whole:
-        bounds = [min(reach, n_blocks // 2) for reach in bounds]
+        bounds = [min(reach, (window - cells + 1) // 2) for reach in bounds]
     for reach in sorted(set(bounds), reverse=True):
         lefts = [left for left in range(MAXDEG) if bounds[left] == reach]
         levels(lefts[0], lefts[-1], reach)
     out_ref[...] = fields[0][pl.ds(RADIUS + home * cells, cells)]
 
 
-def combine_kernel(masks, owners_ref, mine_ref, theirs_ref, *refs):
-    panels, outs = refs[: len(masks)], refs[len(masks) :]
-    me = lax.axis_index("orb")
-    for out, coefficients in zip(outs, (mine_ref, theirs_ref)):
+def combine_kernel(count, weights_ref, *refs):
+    panels, outs = refs[:count], refs[count:]
+    for out, ref in enumerate(outs):
         total = None
-        for mask, panel in zip(masks, panels):
-            weight = jnp.float32(0)
-            for step in range(STEPS):
-                weight = weight + jnp.where(owners_ref[step] == me ^ mask, coefficients[step], 0.0)
-            term = weight * panel[...]
+        for index, panel in enumerate(panels):
+            term = weights_ref[out, index : index + 1] * panel[...]
             total = term if total is None else total + term
-        out[...] = total
+        ref[...] = total
 
 
 def in_vmem(x):
@@ -178,56 +171,62 @@
     if whole:
         slots = list(range(n_dom))
         window = n_dom * cells
-        counts = range(1, n_dom + 1)
+        extents = {min(cells + 2 * RADIUS * left, window) for left in range(MAXDEG)}
     else:
         slots = [0] + [s * k for k in range(1, halo + 1) for s in (1, -1)]
         window = (2 * halo + 1) * cells
-        counts = [1]
+        extents = {cells}
     high, low = ring(width, 1)
     across = np.block([[high, low], [high, low]])
-    groups = sorted({max(g for g in range(1, width // planes + 1) if c * cells % (2 * g) == 0) for c in counts})
+    groups = sorted({max(g for g in range(1, width // planes + 1) if e % (2 * g) == 0) for e in extents})
     alongs = [np.block([[m, m] for m in ring(planes, g)]) for g in groups]
     field = pltpu.VMEM((window + 2 * RADIUS, planes, width), jnp.float32)
     vmem = pl.BlockSpec(memory_space=pltpu.VMEM)
     smem = pl.BlockSpec(memory_space=pltpu.SMEM)
+    operands = [jnp.asarray(m) for m in [across] + alongs] + blocks
     return pl.pallas_call(
         functools.partial(chain_kernel, whole, slots, groups, n_dom),
         out_shape=pltpu.VMEM((cells, planes, width), jnp.float32),
-        in_specs=[smem] + [vmem] * (1 + len(groups) + len(slots)),
+        in_specs=[smem] + [vmem] * len(operands),
         out_specs=vmem,
         scratch_shapes=[field, field, pltpu.VMEM((window, planes, width), jnp.float32)],
-    )(degree, *[in_vmem(b) for b in [jnp.asarray(m) for m in [across] + alongs] + blocks])
+    )(degree, *[in_vmem(x) for x in operands])
 
 
 def per_device(orbitals, potential, degree, owners, rotation):
     _, planes, cells, width = orbitals.shape
     n_dom = lax.axis_size("dom")
     n_orb = lax.axis_size("orb")
+    me = lax.axis_index("orb")
     vmem = pl.BlockSpec(memory_space=pltpu.VMEM)
-    smem = pl.BlockSpec(memory_space=pltpu.SMEM)
     f32 = jnp.float32
     slab = pltpu.VMEM((cells, planes, width), f32)
 
     orbital = jnp.transpose(orbitals[0], (1, 0, 2)).astype(f32)
-    packed = jnp.concatenate([orbital, jnp.transpose(potential, (1, 0, 2))], 0)
-
+    potential = jnp.transpose(potential, (1, 0, 2))
+    packed = jnp.concatenate([orbital, potential], 0)
     halo = -(-RADIUS * MAXDEG // cells)
     if n_dom <= 2 * halo + 1:
         pairs = [xor_pairs(n_dom, k) for k in range(1, n_dom)]
     else:
         pairs = [shift_pairs(n_dom, s * k) for k in range(1, halo + 1) for s in (1, -1)]
-    panel = chain(degree, [packed] + [lax.ppermute(packed, "dom", p) for p in pairs], n_dom)
+    arrived = [lax.ppermute(packed, "dom", p) for p in pairs]
+    panel = chain(degree, [packed] + arrived, n_dom)
 
     coefficients = rotation[:, 0, 0].astype(f32)
     beside = lax.ppermute(coefficients, "orb", xor_pairs(n_orb, 1))
-    masks = sorted(range(2, n_orb, 2), key=lambda m: -m)
+    masks = sorted(range(2, n_orb, 2), key=lambda m: (m % 4 == 2, m))
     panels = [panel] + [lax.ppermute(panel, "orb", xor_pairs(n_orb, m)) for m in masks]
+    held = jnp.stack([me ^ m for m in [0] + masks])
+    chosen = (owners[:, None] == held[None, :]).astype(f32)
+    weights = jnp.stack([jnp.sum(c[:, None] * chosen, 0) for c in (coefficients, beside)])
+    weights = jnp.broadcast_to(weights[:, :, None], weights.shape + (width,))
     mine, theirs = pl.pallas_call(
-        functools.partial(combine_kernel, [0] + masks),
+        functools.partial(combine_kernel, len(panels)),
         out_shape=(slab, slab),
-        in_specs=[smem] * 3 + [vmem] * len(panels),
+        in_specs=[vmem] * (1 + len(panels)),
         out_specs=(vmem, vmem),
-    )(owners, coefficients, beside, *[in_vmem(p) for p in panels])
+    )(in_vmem(weights), *[in_vmem(p) for p in panels])
     rotated = mine + lax.ppermute(theirs, "orb", xor_pairs(n_orb, 1))
     return tuple(jnp.transpose(x, (1, 0, 2))[None] for x in (panel, rotated))
 

time: 32.3 us -> 30.7 us (0.950); the launches traced: 32.1 us -> 30.9 us
  starting transfers between devices: 12.1 us -> 9.12 us
  Pallas kernels: 1.13 us -> 3.4 us
  waiting for transfers between devices: 15.3 us -> 14.3 us
    ppermute x3, starting transfers between devices: 7.47 us -> 4.45 us  [per_device(): lax.ppermute(panel, 'orb', xor_pairs(n_orb, m))]
    pallas_call x1, Pallas kernels: 0.38 us -> 3.34 us  [chain(): pl.pallas_call(functools.partial(chain_kernel, whole, slots, groups, n_do...]
    ppermute x3, waiting for transfers between devices: 8.37 us -> 7.57 us  [per_device(): arrived = [lax.ppermute(packed, 'dom', p) for p in pairs]]
    ppermute x1, waiting for transfers between devices: 1.11 us -> 0.37 us  [per_device(): beside = lax.ppermute(coefficients, 'orb', xor_pairs(n_orb, 1))]
    pallas_call x1, Pallas kernels: 0.75 us -> 0.06 us  [per_device(): pl.pallas_call(functools.partial(combine_kernel, len(panels)), out_shape=...]
    ppermute x3, waiting for transfers between devices: 5.19 us -> 5.72 us  [per_device(): lax.ppermute(panel, 'orb', xor_pairs(n_orb, m))]
    unnamed x15 -> x13, local copies, waits for them, and re-layouts: 0.74 us -> 0.93 us
  transfers between devices with their start and end apart: 8 -> 8, of which waited for: 6 -> 7; matrix products, arithmetic and copies ran while one was open for 2% -> 3% of each run, Pallas kernels for 0% -> 0%
where the time goes in v2:
time: 30.7 us; the launch traced here: 30.9 us
  waiting for transfers between devices  14.3 us (47%)
  starting transfers between devices  9.12 us (30%)
  Pallas kernels  3.4 us (11%)
  other arithmetic  1.68 us (5%)
  between operations  1.36 us (4%)
  local copies, waits for them, and re-layouts  1 us (3%)
    ppermute x3, waiting for transfers between devices, per_device(): arrived = [lax.ppermute(packed, 'dom', p) for p in pairs]  7.57 us
    ppermute x3, waiting for transfers between devices, per_device(): lax.ppermute(panel, 'orb', xor_pairs(n_orb, m))  5.72 us
    ppermute x3, starting transfers between devices, per_device(): arrived = [lax.ppermute(packed, 'dom', p) for p in pairs]  4.54 us
    ppermute x3, starting transfers between devices, per_device(): lax.ppermute(panel, 'orb', xor_pairs(n_orb, m))  4.45 us
    pallas_call x1, Pallas kernels, chain(): pl.pallas_call(functools.partial(chain_kernel, whole, slots, groups, n_do...  3.34 us
    unnamed x13, local copies, waits for them, and re-layouts  0.93 us
    convert_element_type x1, other arithmetic, per_device(): orbital = jnp.transpose(orbitals[0], (1, 0, 2)).astype(f32)  0.84 us
    broadcast_in_dim x1, other arithmetic, per_device(): return tuple((jnp.transpose(x, (1, 0, 2))[None] for x in (panel, rotated)))  0.65 us
  transfers between devices with their start and end apart: 8, of which 7 were waited for; matrix products, arithmetic and copies ran while one was open for 3% of the time, Pallas kernels for 0%

profile of v2, /device:TPU:0, one launch (start us, length us, event | category | flops | bytes accessed | tf_op | source)
XLA Modules:
  0.0 30.9 jit_solution(14287678268883718331)
XLA Ops:
  0.6 0.0 copy-start.3
  0.6 0.8 %convert_bitcast_fusion = f32[12,16,128]{2,1,0:T(8,128)S(1)} fusion(bf16[1,16,12,128]{3,1,2,0:T(8,128)(2,1)} %param.8), kind=kLoop, calls=%fused_computation.1 | loop fusion | flops 24576 | bytes 147456 | tf_op jit(solution)/shard_map/convert_element_type | solution.py:205
  1.5 0.1 copy-done.3
  1.5 0.0 copy-start.5
  1.5 0.0 copy-start
  1.6 0.0 copy-start.1
  1.6 0.0 copy-start.2
  1.6 3.0 %collective-permute-start = (f32[24,16,128]{2,1,0:T(8,128)S(1)}, f32[24,16,128]{2,1,0:T(8,128)S(1)}, u32[]{:S(2)}, u32[]{:S(2)}) collective-permute-start(f32[24,16,128]{2,1,0:T(8,128)S(1)} %pad_maximum_fusion.refs_2_), channel_id=1, source_target_pairs={{0,1},{1,0},{2,3},{3,2},{4,5},{5,4},{6,7},{7,6},{8,9},{9,8},{10,11... | collective-permute-start | bytes 589832 | tf_op jit(solution)/shard_map/ppermute | solution.py:213
  4.6 1.5 %collective-permute-start.1 = (f32[24,16,128]{2,1,0:T(8,128)S(1)}, f32[24,16,128]{2,1,0:T(8,128)S(1)}, u32[]{:S(2)}, u32[]{:S(2)}) collective-permute-start(f32[24,16,128]{2,1,0:T(8,128)S(1)} %pad_maximum_fusion.refs_2_), channel_id=1, source_target_pairs={{0,2},{1,3},{2,0},{3,1},{4,6},{5,7},{6,4},{7,5},{8,10},{9,11},{10,... | collective-permute-start | bytes 589832 | tf_op jit(solution)/shard_map/ppermute | solution.py:213
  6.1 0.0 collective-permute-start.2
  6.1 0.0 copy-done.5
  6.1 0.1 collective-permute-start.3
  6.8 0.0 copy-start.4
  6.9 0.1 pad_add_fusion
  6.9 0.4 %collective-permute-done.3 = f32[4]{0:T(128)S(1)} collective-permute-done((f32[4]{0:T(128)S(1)}, f32[4]{0:T(128)S(1)}, u32[]{:S(2)}, u32[]{:S(2)}) %collective-permute-start.3) | collective-permute-done | bytes 48 | tf_op jit(solution)/shard_map/ppermute | solution.py:217
  7.3 0.2 copy-done.4
  7.5 0.1 fusion
  7.6 2.7 %collective-permute-done.refs_3_ = f32[24,16,128]{2,1,0:T(8,128)S(1)} collective-permute-done((f32[24,16,128]{2,1,0:T(8,128)S(1)}, f32[24,16,128]{2,1,0:T(8,128)S(1)}, u32[]{:S(2)}, u32[]{:S(2)}) %collective-permute-start) | collective-permute-done | bytes 196640 | tf_op jit(solution)/shard_map/ppermute | solution.py:213
  10.3 4.8 %collective-permute-done.1.refs_4_ = f32[24,16,128]{2,1,0:T(8,128)S(1)} collective-permute-done((f32[24,16,128]{2,1,0:T(8,128)S(1)}, f32[24,16,128]{2,1,0:T(8,128)S(1)}, u32[]{:S(2)}, u32[]{:S(2)}) %collective-permute-start.1) | collective-permute-done | bytes 196640 | tf_op jit(solution)/shard_map/ppermute | solution.py:213
  15.2 0.0 collective-permute-done.2.refs_5_
  15.2 0.0 copy-done
  15.2 0.0 copy-done.1
  15.2 0.0 copy-done.2
  15.2 3.3 %shard_map.95.refs_0_ = f32[12,16,128]{2,1,0:T(8,128)S(1)} custom-call(s32[1]{0:T(128)S(6)} %copy.11.degree_ref, bf16[256,256]{1,0:T(8,128)(2,1)S(1)} %copy-done, bf16[192,192]{1,0:T(8,128)(2,1)S(1)} %copy-done.2, bf16[256,256]{1,0:T(8,128)(2,1)S(1)} %copy-done.1, f32[24,16,128]{2,1,0:T(8,128)S(1)} %pad_maximum_fusion.refs_2_, ...), custom_call_target="tpu_custom_call" | custom-call | tf_op jit(solution)/shard_map/pallas_call | solution.py:187
  18.5 0.3 %collective-permute-start.4 = (f32[12,16,128]{2,1,0:T(8,128)S(1)}, f32[12,16,128]{2,1,0:T(8,128)S(1)}, u32[]{:S(2)}, u32[]{:S(2)}) collective-permute-start(f32[12,16,128]{2,1,0:T(8,128)S(1)} %shard_map.95.refs_0_), channel_id=1, source_target_pairs={{0,16},{4,20},{8,24},{12,28},{16,0},{20,4},{24,8},{28,12},{1,17},{... | collective-permute-start | bytes 294920 | tf_op jit(solution)/shard_map/ppermute | solution.py:219
  18.9 3.4 %collective-permute-start.5 = (f32[12,16,128]{2,1,0:T(8,128)S(1)}, f32[12,16,128]{2,1,0:T(8,128)S(1)}, u32[]{:S(2)}, u32[]{:S(2)}) collective-permute-start(f32[12,16,128]{2,1,0:T(8,128)S(1)} %shard_map.95.refs_0_), channel_id=1, source_target_pairs={{0,8},{4,12},{8,0},{12,4},{16,24},{20,28},{24,16},{28,20},{1,9},{5... | collective-permute-start | bytes 294920 | tf_op jit(solution)/shard_map/ppermute | solution.py:219
  22.3 0.7 %collective-permute-start.6 = (f32[12,16,128]{2,1,0:T(8,128)S(1)}, f32[12,16,128]{2,1,0:T(8,128)S(1)}, u32[]{:S(2)}, u32[]{:S(2)}) collective-permute-start(f32[12,16,128]{2,1,0:T(8,128)S(1)} %shard_map.95.refs_0_), channel_id=1, source_target_pairs={{0,24},{4,28},{8,16},{12,20},{16,8},{20,12},{24,0},{28,4},{1,25},{... | collective-permute-start | bytes 294920 | tf_op jit(solution)/shard_map/ppermute | solution.py:219
  23.0 3.3 %collective-permute-done.4.refs_1_ = f32[12,16,128]{2,1,0:T(8,128)S(1)} collective-permute-done((f32[12,16,128]{2,1,0:T(8,128)S(1)}, f32[12,16,128]{2,1,0:T(8,128)S(1)}, u32[]{:S(2)}, u32[]{:S(2)}) %collective-permute-start.4) | collective-permute-done | bytes 98336 | tf_op jit(solution)/shard_map/ppermute | solution.py:219
  26.3 0.2 collective-permute-done.5.refs_2_
  26.5 2.2 %collective-permute-done.6.refs_3_ = f32[12,16,128]{2,1,0:T(8,128)S(1)} collective-permute-done((f32[12,16,128]{2,1,0:T(8,128)S(1)}, f32[12,16,128]{2,1,0:T(8,128)S(1)}, u32[]{:S(2)}, u32[]{:S(2)}) %collective-permute-start.6) | collective-permute-done | bytes 98336 | tf_op jit(solution)/shard_map/ppermute | solution.py:219
  28.7 0.1 broadcast_in_dim.7.weights_ref
  28.8 0.1 shard_map.96
  28.8 0.1 collective-permute-start.7
  28.9 0.6 %copy.10 = f32[1,16,12,128]{3,1,2,0:T(8,128)} copy(f32[1,16,12,128]{3,1,2,0:T(8,128)S(1)} %bitcast.22) | data formatting | bytes 196608
  29.6 0.6 %collective-permute-done.7 = f32[12,16,128]{2,1,0:T(8,128)S(1)} collective-permute-done((f32[12,16,128]{2,1,0:T(8,128)S(1)}, f32[12,16,128]{2,1,0:T(8,128)S(1)}, u32[]{:S(2)}, u32[]{:S(2)}) %collective-permute-start.7) | collective-permute-done | bytes 98336 | tf_op jit(solution)/shard_map/ppermute | solution.py:230
  30.2 0.7 %add_bitcast_fusion = f32[1,16,12,128]{3,1,2,0:T(8,128)} fusion(f32[12,16,128]{2,1,0:T(8,128)S(1)} %get-tuple-element.4, f32[12,16,128]{2,1,0:T(8,128)S(1)} %collective-permute-done.7), kind=kLoop, calls=%fused_computation.2 | loop fusion | flops 24576 | bytes 294912 | tf_op jit(solution)/shard_map/broadcast_in_dim | solution.py:231
  (3 shorter events, 0.0 us)
Async XLA Ops:
  0.6 0.9 %copy-start.3 = (f32[16,12,128]{2,0,1:T(8,128)S(1)}, f32[16,12,128]{2,0,1:T(8,128)}, u32[]{:S(2)}) copy-start(f32[16,12,128]{2,0,1:T(8,128)} %param.9) | copy-start | bytes 294916
  1.5 4.6 %copy-start.5 = (bf16[4,1,1]{0,2,1:T(2,128)(2,1)S(1)}, bf16[4,1,1]{0,2,1:T(2,128)(2,1)}, u32[]{:S(2)}) copy-start(bf16[4,1,1]{0,2,1:T(2,128)(2,1)} %param.12) | copy-start | bytes 28
  1.5 13.6 %copy-start = (bf16[256,256]{1,0:T(8,128)(2,1)S(1)}, bf16[256,256]{1,0:T(8,128)(2,1)}, u32[]{:S(2)}) copy-start(bf16[256,256]{1,0:T(8,128)(2,1)} %constant.22.clone.rows_ref) | copy-start | bytes 393220
  1.6 13.6 %copy-start.1 = (bf16[256,256]{1,0:T(8,128)(2,1)S(1)}, bf16[256,256]{1,0:T(8,128)(2,1)}, u32[]{:S(2)}) copy-start(bf16[256,256]{1,0:T(8,128)(2,1)} %constant.24.clone.refs_1_) | copy-start | bytes 393220
  1.6 13.6 %copy-start.2 = (bf16[192,192]{1,0:T(8,128)(2,1)S(1)}, bf16[192,192]{1,0:T(8,128)(2,1)}, u32[]{:S(2)}) copy-start(bf16[192,192]{1,0:T(8,128)(2,1)} %constant.23.clone.refs_0_) | copy-start | bytes 221188
  1.6 8.7 %collective-permute-start = (f32[24,16,128]{2,1,0:T(8,128)S(1)}, f32[24,16,128]{2,1,0:T(8,128)S(1)}, u32[]{:S(2)}, u32[]{:S(2)}) collective-permute-start(f32[24,16,128]{2,1,0:T(8,128)S(1)} %pad_maximum_fusion.refs_2_), channel_id=1, source_target_pairs={{0,1},{1,0},{2,3},{3,2},{4,5},{5,4},{6,7},{7,6},{8,9},{9,8},{10,11... | collective-permute-start | bytes 589832 | tf_op jit(solution)/shard_map/ppermute | solution.py:213
  4.6 10.6 %collective-permute-start.1 = (f32[24,16,128]{2,1,0:T(8,128)S(1)}, f32[24,16,128]{2,1,0:T(8,128)S(1)}, u32[]{:S(2)}, u32[]{:S(2)}) collective-permute-start(f32[24,16,128]{2,1,0:T(8,128)S(1)} %pad_maximum_fusion.refs_2_), channel_id=1, source_target_pairs={{0,2},{1,3},{2,0},{3,1},{4,6},{5,7},{6,4},{7,5},{8,10},{9,11},{10,... | collective-permute-start | bytes 589832 | tf_op jit(solution)/shard_map/ppermute | solution.py:213
  6.1 9.1 %collective-permute-start.2 = (f32[24,16,128]{2,1,0:T(8,128)S(1)}, f32[24,16,128]{2,1,0:T(8,128)S(1)}, u32[]{:S(2)}, u32[]{:S(2)}) collective-permute-start(f32[24,16,128]{2,1,0:T(8,128)S(1)} %pad_maximum_fusion.refs_2_), channel_id=1, source_target_pairs={{0,3},{1,2},{2,1},{3,0},{4,7},{5,6},{6,5},{7,4},{8,11},{9,10},{10,... | collective-permute-start | bytes 589832 | tf_op jit(solution)/shard_map/ppermute | solution.py:213
  6.1 1.2 %collective-permute-start.3 = (f32[4]{0:T(128)S(1)}, f32[4]{0:T(128)S(1)}, u32[]{:S(2)}, u32[]{:S(2)}) collective-permute-start(f32[4]{0:T(128)S(1)} %bitcast_convert_fusion), channel_id=1, source_target_pairs={{0,4},{4,0},{8,12},{12,8},{16,20},{20,16},{24,28},{28,24},{1,5},{5... | collective-permute-start | bytes 56 | tf_op jit(solution)/shard_map/ppermute | solution.py:217
  6.8 0.7 %copy-start.4 = (s32[4]{0:T(128)S(1)}, s32[4]{0:T(128)}, u32[]{:S(2)}) copy-start(s32[4]{0:T(128)} %param.11) | copy-start | bytes 52
  18.5 7.8 %collective-permute-start.4 = (f32[12,16,128]{2,1,0:T(8,128)S(1)}, f32[12,16,128]{2,1,0:T(8,128)S(1)}, u32[]{:S(2)}, u32[]{:S(2)}) collective-permute-start(f32[12,16,128]{2,1,0:T(8,128)S(1)} %shard_map.95.refs_0_), channel_id=1, source_target_pairs={{0,16},{4,20},{8,24},{12,28},{16,0},{20,4},{24,8},{28,12},{1,17},{... | collective-permute-start | bytes 294920 | tf_op jit(solution)/shard_map/ppermute | solution.py:219
  18.9 7.7 %collective-permute-start.5 = (f32[12,16,128]{2,1,0:T(8,128)S(1)}, f32[12,16,128]{2,1,0:T(8,128)S(1)}, u32[]{:S(2)}, u32[]{:S(2)}) collective-permute-start(f32[12,16,128]{2,1,0:T(8,128)S(1)} %shard_map.95.refs_0_), channel_id=1, source_target_pairs={{0,8},{4,12},{8,0},{12,4},{16,24},{20,28},{24,16},{28,20},{1,9},{5... | collective-permute-start | bytes 294920 | tf_op jit(solution)/shard_map/ppermute | solution.py:219
  22.3 6.4 %collective-permute-start.6 = (f32[12,16,128]{2,1,0:T(8,128)S(1)}, f32[12,16,128]{2,1,0:T(8,128)S(1)}, u32[]{:S(2)}, u32[]{:S(2)}) collective-permute-start(f32[12,16,128]{2,1,0:T(8,128)S(1)} %shard_map.95.refs_0_), channel_id=1, source_target_pairs={{0,24},{4,28},{8,16},{12,20},{16,8},{20,12},{24,0},{28,4},{1,25},{... | collective-permute-start | bytes 294920 | tf_op jit(solution)/shard_map/ppermute | solution.py:219
  28.8 1.4 %collective-permute-start.7 = (f32[12,16,128]{2,1,0:T(8,128)S(1)}, f32[12,16,128]{2,1,0:T(8,128)S(1)}, u32[]{:S(2)}, u32[]{:S(2)}) collective-permute-start(f32[12,16,128]{2,1,0:T(8,128)S(1)} %get-tuple-element.5), channel_id=1, source_target_pairs={{0,4},{4,0},{8,12},{12,8},{16,20},{20,16},{24,28},{28,24},{1,5},{5... | collective-permute-start | bytes 294920 | tf_op jit(solution)/shard_map/ppermute | solution.py:230

commit v3 on v2

--- a/solution.py
+++ b/solution.py
@@ -42,13 +42,14 @@
     return high, (values - high.astype(jnp.float32)).astype(jnp.bfloat16)
 
 
-def ring(count, copies):
-    matrix = np.zeros((count, count), np.float64)
+def stencil(count, cells):
+    around = np.zeros((count, count), np.float64)
     for k, tap in enumerate(TAPS, 1):
         for i in range(count):
-            matrix[i, (i + k) % count] += tap
-            matrix[i, (i - k) % count] += tap
-    matrix = np.kron(np.eye(copies), matrix)
+            around[i, (i + k) % count] += tap
+            around[i, (i - k) % count] += tap
+    between = sum(tap * (np.eye(cells, k=k) + np.eye(cells, k=-k)) for k, tap in enumerate(TAPS, 1))
+    matrix = np.kron(np.eye(cells), around) + np.kron(between, np.eye(count))
     high = matrix.astype(ml_dtypes.bfloat16)
     low = (matrix - high.astype(np.float64)).astype(ml_dtypes.bfloat16)
     return high, low
@@ -96,15 +97,17 @@
                     planes_at[group][...], jnp.concatenate(pieces, 0), preferred_element_type=jnp.float32
                 )
             )
-        for part in range(0, extent, RADIUS):
-            x = base + part
-            near = source[pl.ds(x, 3 * RADIUS)]
-            total = potential[pl.ds(x, RADIUS)] * near[RADIUS : 2 * RADIUS]
-            for k in range(1, RADIUS + 1):
-                beside = near[RADIUS + k : 2 * RADIUS + k] + near[RADIUS - k : 2 * RADIUS - k]
-                total = total + TAPS[k - 1] * beside
-            spot = pl.ds(RADIUS + x, RADIUS)
-            target[spot] = factor * total - target[spot]
+        for tile in range(0, extent, group):
+            x = RADIUS + base + tile
+            below = [source[x - RADIUS + j] for j in range(RADIUS)]
+            above = [source[x + group + j] for j in range(RADIUS)]
+            for i in range(group):
+                total = potential[x - RADIUS + i] * source[x + i] - target[x + i]
+                for k in range(1, RADIUS + 1):
+                    outside = ([below[RADIUS + i - k]] if i < k else []) + ([above[i + k - group]] if i + k >= group else [])
+                    if outside:
+                        total = total + TAPS[k - 1] * functools.reduce(jnp.add, outside)
+                target[x + i] = total
         for index, along in enumerate(alongs):
             along = along[:size] + along[size:]
             for half in range(2):
@@ -112,7 +115,7 @@
                 plane_sum = across[top : top + size, :width] + across[top : top + size, width:]
                 plane_sum = plane_sum + along[:, half * width : (half + 1) * width]
                 spot = pl.ds(RADIUS + base + (2 * index + half) * group, group)
-                target[spot] = target[spot] + factor * plane_sum.reshape(group, planes, width)
+                target[spot] = factor * (target[spot] + plane_sum.reshape(group, planes, width))
 
     def level(left, parity, reach):
         factor = jnp.where(left == degree - 1, 0.5, 1.0)
@@ -176,10 +179,10 @@
         slots = [0] + [s * k for k in range(1, halo + 1) for s in (1, -1)]
         window = (2 * halo + 1) * cells
         extents = {cells}
-    high, low = ring(width, 1)
+    high, low = stencil(width, 1)
     across = np.block([[high, low], [high, low]])
     groups = sorted({max(g for g in range(1, width // planes + 1) if e % (2 * g) == 0) for e in extents})
-    alongs = [np.block([[m, m] for m in ring(planes, g)]) for g in groups]
+    alongs = [np.block([[m, m] for m in stencil(planes, g)]) for g in groups]
     field = pltpu.VMEM((window + 2 * RADIUS, planes, width), jnp.float32)
     vmem = pl.BlockSpec(memory_space=pltpu.VMEM)
     smem = pl.BlockSpec(memory_space=pltpu.SMEM)

time: 30.7 us -> 30.4 us (level)
  Pallas kernels: 3.4 us -> 2.02 us
  waiting for transfers between devices: 14.3 us -> 15.1 us
  starting transfers between devices: 9.12 us -> 9.51 us
    pallas_call x1, Pallas kernels: 3.34 us -> 1.96 us  [chain(): pl.pallas_call(functools.partial(chain_kernel, whole, slots, groups, n_do...]
    ppermute x3, waiting for transfers between devices: 5.72 us -> 6.49 us  [per_device(): lax.ppermute(panel, 'orb', xor_pairs(n_orb, m))]
    ppermute x3, starting transfers between devices: 4.45 us -> 4.84 us  [per_device(): lax.ppermute(panel, 'orb', xor_pairs(n_orb, m))]
where the time goes in v3:
time: 30.4 us; the launch traced here: 30.6 us
  waiting for transfers between devices  15.1 us (50%)
  starting transfers between devices  9.51 us (31%)
  Pallas kernels  2.02 us (7%)
  other arithmetic  1.68 us (6%)
  between operations  1.36 us (4%)
  local copies, waits for them, and re-layouts  1 us (3%)
    ppermute x3, waiting for transfers between devices, per_device(): arrived = [lax.ppermute(packed, 'dom', p) for p in pairs]  7.57 us
    ppermute x3, waiting for transfers between devices, per_device(): lax.ppermute(panel, 'orb', xor_pairs(n_orb, m))  6.49 us
    ppermute x3, starting transfers between devices, per_device(): lax.ppermute(panel, 'orb', xor_pairs(n_orb, m))  4.84 us
    ppermute x3, starting transfers between devices, per_device(): arrived = [lax.ppermute(packed, 'dom', p) for p in pairs]  4.54 us
    pallas_call x1, Pallas kernels, chain(): pl.pallas_call(functools.partial(chain_kernel, whole, slots, groups, n_do...  1.96 us
    unnamed x13, local copies, waits for them, and re-layouts  0.93 us
    convert_element_type x1, other arithmetic, per_device(): orbital = jnp.transpose(orbitals[0], (1, 0, 2)).astype(f32)  0.84 us
    broadcast_in_dim x1, other arithmetic, per_device(): return tuple((jnp.transpose(x, (1, 0, 2))[None] for x in (panel, rotated)))  0.65 us
  transfers between devices with their start and end apart: 8, of which 7 were waited for; matrix products, arithmetic and copies ran while one was open for 3% of the time, Pallas kernels for 0%

profile of v3, /device:TPU:0, one launch (start us, length us, event | category | flops | bytes accessed | tf_op | source)
XLA Modules:
  0.0 30.6 jit_solution(10623334024407211558)
XLA Ops:
  0.6 0.0 copy-start.3
  0.6 0.8 %convert_bitcast_fusion = f32[12,16,128]{2,1,0:T(8,128)S(1)} fusion(bf16[1,16,12,128]{3,1,2,0:T(8,128)(2,1)} %param.8), kind=kLoop, calls=%fused_computation.1 | loop fusion | flops 24576 | bytes 147456 | tf_op jit(solution)/shard_map/convert_element_type | solution.py:208
  1.5 0.1 copy-done.3
  1.5 0.0 copy-start.5
  1.5 0.0 copy-start
  1.6 0.0 copy-start.1
  1.6 0.0 copy-start.2
  1.6 3.0 %collective-permute-start = (f32[24,16,128]{2,1,0:T(8,128)S(1)}, f32[24,16,128]{2,1,0:T(8,128)S(1)}, u32[]{:S(2)}, u32[]{:S(2)}) collective-permute-start(f32[24,16,128]{2,1,0:T(8,128)S(1)} %pad_maximum_fusion.refs_2_), channel_id=1, source_target_pairs={{0,1},{1,0},{2,3},{3,2},{4,5},{5,4},{6,7},{7,6},{8,9},{9,8},{10,11... | collective-permute-start | bytes 589832 | tf_op jit(solution)/shard_map/ppermute | solution.py:216
  4.6 1.5 %collective-permute-start.1 = (f32[24,16,128]{2,1,0:T(8,128)S(1)}, f32[24,16,128]{2,1,0:T(8,128)S(1)}, u32[]{:S(2)}, u32[]{:S(2)}) collective-permute-start(f32[24,16,128]{2,1,0:T(8,128)S(1)} %pad_maximum_fusion.refs_2_), channel_id=1, source_target_pairs={{0,2},{1,3},{2,0},{3,1},{4,6},{5,7},{6,4},{7,5},{8,10},{9,11},{10,... | collective-permute-start | bytes 589832 | tf_op jit(solution)/shard_map/ppermute | solution.py:216
  6.1 0.0 collective-permute-start.2
  6.1 0.0 copy-done.5
  6.1 0.1 collective-permute-start.3
  6.8 0.0 copy-start.4
  6.9 0.1 pad_add_fusion
  6.9 0.4 %collective-permute-done.3 = f32[4]{0:T(128)S(1)} collective-permute-done((f32[4]{0:T(128)S(1)}, f32[4]{0:T(128)S(1)}, u32[]{:S(2)}, u32[]{:S(2)}) %collective-permute-start.3) | collective-permute-done | bytes 48 | tf_op jit(solution)/shard_map/ppermute | solution.py:220
  7.3 0.2 copy-done.4
  7.5 0.1 fusion
  7.6 2.7 %collective-permute-done.refs_3_ = f32[24,16,128]{2,1,0:T(8,128)S(1)} collective-permute-done((f32[24,16,128]{2,1,0:T(8,128)S(1)}, f32[24,16,128]{2,1,0:T(8,128)S(1)}, u32[]{:S(2)}, u32[]{:S(2)}) %collective-permute-start) | collective-permute-done | bytes 196640 | tf_op jit(solution)/shard_map/ppermute | solution.py:216
  10.3 4.8 %collective-permute-done.1.refs_4_ = f32[24,16,128]{2,1,0:T(8,128)S(1)} collective-permute-done((f32[24,16,128]{2,1,0:T(8,128)S(1)}, f32[24,16,128]{2,1,0:T(8,128)S(1)}, u32[]{:S(2)}, u32[]{:S(2)}) %collective-permute-start.1) | collective-permute-done | bytes 196640 | tf_op jit(solution)/shard_map/ppermute | solution.py:216
  15.2 0.0 collective-permute-done.2.refs_5_
  15.2 0.0 copy-done
  15.2 0.0 copy-done.1
  15.2 0.0 copy-done.2
  15.2 2.0 %shard_map.95.refs_0_ = f32[12,16,128]{2,1,0:T(8,128)S(1)} custom-call(s32[1]{0:T(128)S(6)} %copy.11.degree_ref, bf16[256,256]{1,0:T(8,128)(2,1)S(1)} %copy-done, bf16[192,192]{1,0:T(8,128)(2,1)S(1)} %copy-done.2, bf16[256,256]{1,0:T(8,128)(2,1)S(1)} %copy-done.1, f32[24,16,128]{2,1,0:T(8,128)S(1)} %pad_maximum_fusion.refs_2_, ...), custom_call_target="tpu_custom_call" | custom-call | tf_op jit(solution)/shard_map/pallas_call | solution.py:190
  17.1 3.3 %collective-permute-start.4 = (f32[12,16,128]{2,1,0:T(8,128)S(1)}, f32[12,16,128]{2,1,0:T(8,128)S(1)}, u32[]{:S(2)}, u32[]{:S(2)}) collective-permute-start(f32[12,16,128]{2,1,0:T(8,128)S(1)} %shard_map.95.refs_0_), channel_id=1, source_target_pairs={{0,16},{4,20},{8,24},{12,28},{16,0},{20,4},{24,8},{28,12},{1,17},{... | collective-permute-start | bytes 294920 | tf_op jit(solution)/shard_map/ppermute | solution.py:222
  20.4 1.6 %collective-permute-start.5 = (f32[12,16,128]{2,1,0:T(8,128)S(1)}, f32[12,16,128]{2,1,0:T(8,128)S(1)}, u32[]{:S(2)}, u32[]{:S(2)}) collective-permute-start(f32[12,16,128]{2,1,0:T(8,128)S(1)} %shard_map.95.refs_0_), channel_id=1, source_target_pairs={{0,8},{4,12},{8,0},{12,4},{16,24},{20,28},{24,16},{28,20},{1,9},{5... | collective-permute-start | bytes 294920 | tf_op jit(solution)/shard_map/ppermute | solution.py:222
  22.0 0.0 collective-permute-start.6
  22.0 4.2 %collective-permute-done.4.refs_1_ = f32[12,16,128]{2,1,0:T(8,128)S(1)} collective-permute-done((f32[12,16,128]{2,1,0:T(8,128)S(1)}, f32[12,16,128]{2,1,0:T(8,128)S(1)}, u32[]{:S(2)}, u32[]{:S(2)}) %collective-permute-start.4) | collective-permute-done | bytes 98336 | tf_op jit(solution)/shard_map/ppermute | solution.py:222
  26.2 0.2 collective-permute-done.5.refs_2_
  26.4 2.0 %collective-permute-done.6.refs_3_ = f32[12,16,128]{2,1,0:T(8,128)S(1)} collective-permute-done((f32[12,16,128]{2,1,0:T(8,128)S(1)}, f32[12,16,128]{2,1,0:T(8,128)S(1)}, u32[]{:S(2)}, u32[]{:S(2)}) %collective-permute-start.6) | collective-permute-done | bytes 98336 | tf_op jit(solution)/shard_map/ppermute | solution.py:222
  28.5 0.1 broadcast_in_dim.7.weights_ref
  28.6 0.1 shard_map.96
  28.6 0.1 collective-permute-start.7
  28.7 0.6 %copy.10 = f32[1,16,12,128]{3,1,2,0:T(8,128)} copy(f32[1,16,12,128]{3,1,2,0:T(8,128)S(1)} %bitcast.22) | data formatting | bytes 196608
  29.3 0.6 %collective-permute-done.7 = f32[12,16,128]{2,1,0:T(8,128)S(1)} collective-permute-done((f32[12,16,128]{2,1,0:T(8,128)S(1)}, f32[12,16,128]{2,1,0:T(8,128)S(1)}, u32[]{:S(2)}, u32[]{:S(2)}) %collective-permute-start.7) | collective-permute-done | bytes 98336 | tf_op jit(solution)/shard_map/ppermute | solution.py:233
  30.0 0.7 %add_bitcast_fusion = f32[1,16,12,128]{3,1,2,0:T(8,128)} fusion(f32[12,16,128]{2,1,0:T(8,128)S(1)} %get-tuple-element.4, f32[12,16,128]{2,1,0:T(8,128)S(1)} %collective-permute-done.7), kind=kLoop, calls=%fused_computation.2 | loop fusion | flops 24576 | bytes 294912 | tf_op jit(solution)/shard_map/broadcast_in_dim | solution.py:234
  (3 shorter events, 0.0 us)
Async XLA Ops:
  0.6 0.9 %copy-start.3 = (f32[16,12,128]{2,0,1:T(8,128)S(1)}, f32[16,12,128]{2,0,1:T(8,128)}, u32[]{:S(2)}) copy-start(f32[16,12,128]{2,0,1:T(8,128)} %param.9) | copy-start | bytes 294916
  1.5 4.6 %copy-start.5 = (bf16[4,1,1]{0,2,1:T(2,128)(2,1)S(1)}, bf16[4,1,1]{0,2,1:T(2,128)(2,1)}, u32[]{:S(2)}) copy-start(bf16[4,1,1]{0,2,1:T(2,128)(2,1)} %param.12) | copy-start | bytes 28
  1.5 13.6 %copy-start = (bf16[256,256]{1,0:T(8,128)(2,1)S(1)}, bf16[256,256]{1,0:T(8,128)(2,1)}, u32[]{:S(2)}) copy-start(bf16[256,256]{1,0:T(8,128)(2,1)} %constant.22.clone.rows_ref) | copy-start | bytes 393220
  1.6 13.6 %copy-start.1 = (bf16[256,256]{1,0:T(8,128)(2,1)S(1)}, bf16[256,256]{1,0:T(8,128)(2,1)}, u32[]{:S(2)}) copy-start(bf16[256,256]{1,0:T(8,128)(2,1)} %constant.24.clone.refs_1_) | copy-start | bytes 393220
  1.6 13.6 %copy-start.2 = (bf16[192,192]{1,0:T(8,128)(2,1)S(1)}, bf16[192,192]{1,0:T(8,128)(2,1)}, u32[]{:S(2)}) copy-start(bf16[192,192]{1,0:T(8,128)(2,1)} %constant.23.clone.refs_0_) | copy-start | bytes 221188
  1.6 8.7 %collective-permute-start = (f32[24,16,128]{2,1,0:T(8,128)S(1)}, f32[24,16,128]{2,1,0:T(8,128)S(1)}, u32[]{:S(2)}, u32[]{:S(2)}) collective-permute-start(f32[24,16,128]{2,1,0:T(8,128)S(1)} %pad_maximum_fusion.refs_2_), channel_id=1, source_target_pairs={{0,1},{1,0},{2,3},{3,2},{4,5},{5,4},{6,7},{7,6},{8,9},{9,8},{10,11... | collective-permute-start | bytes 589832 | tf_op jit(solution)/shard_map/ppermute | solution.py:216
  4.6 10.6 %collective-permute-start.1 = (f32[24,16,128]{2,1,0:T(8,128)S(1)}, f32[24,16,128]{2,1,0:T(8,128)S(1)}, u32[]{:S(2)}, u32[]{:S(2)}) collective-permute-start(f32[24,16,128]{2,1,0:T(8,128)S(1)} %pad_maximum_fusion.refs_2_), channel_id=1, source_target_pairs={{0,2},{1,3},{2,0},{3,1},{4,6},{5,7},{6,4},{7,5},{8,10},{9,11},{10,... | collective-permute-start | bytes 589832 | tf_op jit(solution)/shard_map/ppermute | solution.py:216
  6.1 9.1 %collective-permute-start.2 = (f32[24,16,128]{2,1,0:T(8,128)S(1)}, f32[24,16,128]{2,1,0:T(8,128)S(1)}, u32[]{:S(2)}, u32[]{:S(2)}) collective-permute-start(f32[24,16,128]{2,1,0:T(8,128)S(1)} %pad_maximum_fusion.refs_2_), channel_id=1, source_target_pairs={{0,3},{1,2},{2,1},{3,0},{4,7},{5,6},{6,5},{7,4},{8,11},{9,10},{10,... | collective-permute-start | bytes 589832 | tf_op jit(solution)/shard_map/ppermute | solution.py:216
  6.1 1.2 %collective-permute-start.3 = (f32[4]{0:T(128)S(1)}, f32[4]{0:T(128)S(1)}, u32[]{:S(2)}, u32[]{:S(2)}) collective-permute-start(f32[4]{0:T(128)S(1)} %bitcast_convert_fusion), channel_id=1, source_target_pairs={{0,4},{4,0},{8,12},{12,8},{16,20},{20,16},{24,28},{28,24},{1,5},{5... | collective-permute-start | bytes 56 | tf_op jit(solution)/shard_map/ppermute | solution.py:220
  6.8 0.7 %copy-start.4 = (s32[4]{0:T(128)S(1)}, s32[4]{0:T(128)}, u32[]{:S(2)}) copy-start(s32[4]{0:T(128)} %param.11) | copy-start | bytes 52
  17.1 9.1 %collective-permute-start.4 = (f32[12,16,128]{2,1,0:T(8,128)S(1)}, f32[12,16,128]{2,1,0:T(8,128)S(1)}, u32[]{:S(2)}, u32[]{:S(2)}) collective-permute-start(f32[12,16,128]{2,1,0:T(8,128)S(1)} %shard_map.95.refs_0_), channel_id=1, source_target_pairs={{0,16},{4,20},{8,24},{12,28},{16,0},{20,4},{24,8},{28,12},{1,17},{... | collective-permute-start | bytes 294920 | tf_op jit(solution)/shard_map/ppermute | solution.py:222
  20.4 6.0 %collective-permute-start.5 = (f32[12,16,128]{2,1,0:T(8,128)S(1)}, f32[12,16,128]{2,1,0:T(8,128)S(1)}, u32[]{:S(2)}, u32[]{:S(2)}) collective-permute-start(f32[12,16,128]{2,1,0:T(8,128)S(1)} %shard_map.95.refs_0_), channel_id=1, source_target_pairs={{0,8},{4,12},{8,0},{12,4},{16,24},{20,28},{24,16},{28,20},{1,9},{5... | collective-permute-start | bytes 294920 | tf_op jit(solution)/shard_map/ppermute | solution.py:222
  22.0 6.5 %collective-permute-start.6 = (f32[12,16,128]{2,1,0:T(8,128)S(1)}, f32[12,16,128]{2,1,0:T(8,128)S(1)}, u32[]{:S(2)}, u32[]{:S(2)}) collective-permute-start(f32[12,16,128]{2,1,0:T(8,128)S(1)} %shard_map.95.refs_0_), channel_id=1, source_target_pairs={{0,24},{4,28},{8,16},{12,20},{16,8},{20,12},{24,0},{28,4},{1,25},{... | collective-permute-start | bytes 294920 | tf_op jit(solution)/shard_map/ppermute | solution.py:222
  28.6 1.4 %collective-permute-start.7 = (f32[12,16,128]{2,1,0:T(8,128)S(1)}, f32[12,16,128]{2,1,0:T(8,128)S(1)}, u32[]{:S(2)}, u32[]{:S(2)}) collective-permute-start(f32[12,16,128]{2,1,0:T(8,128)S(1)} %get-tuple-element.5), channel_id=1, source_target_pairs={{0,4},{4,0},{8,12},{12,8},{16,20},{20,16},{24,28},{28,24},{1,5},{5... | collective-permute-start | bytes 294920 | tf_op jit(solution)/shard_map/ppermute | solution.py:233
